TPU v7x, 512 devices: a whole 4x4x16 slice. The times are simulated.
512 devices in a mesh: ctx: 64 (over x_lo, z, core), tp: 8 (over x_hi, y).
Axes of the slice: x: 4 (x_hi: 2, x_lo: 2; x = x_hi * 2 + x_lo), y: 4, z: 16, core: 2. Of those that a mesh axis runs over, the one named last changes fastest.
Arguments:
- query: bfloat16 [8192, 4096], P('ctx', 'tp'), as said below
- key_proj: bfloat16 [8192, 4096], P('ctx', 'tp'), may hold values from -6 to 6
- value_proj: bfloat16 [8192, 4096], P('ctx', 'tp'), may hold values from -6 to 6
- filter_taps: bfloat16 [8192, 4096], P('ctx', 'tp'), may hold values from -6 to 6
- grad_out: bfloat16 [8192, 4096], P('ctx', 'tp'), may hold values from -6 to 6
Outputs:
- mixer_out: bfloat16 [8192, 4096], P('ctx', 'tp')
- dquery: bfloat16 [8192, 4096], P('ctx', 'tp')
- dkey: bfloat16 [8192, 4096], P('ctx', 'tp')
- dvalue: bfloat16 [8192, 4096], P('ctx', 'tp')
- dtaps: bfloat16 [8192, 4096], P('ctx', 'tp')
Inputs may be any that keep to these rules, and one draw needn't show every extreme that they name: Entries of query are real values of either sign.
All inputs are finite; a program needn't handle non-finite values.
Results may differ from a plain program's by a relative error of at most 0.0085.
Values may be sent and summed in bfloat16 or wider, within the bound.
A program may use at most 64 MiB of HBM per device.

v0:
```python
import math

import jax
import jax.numpy as jnp
from jax import lax
from jax.sharding import PartitionSpec as P

precise = lax.Precision.HIGHEST


def dft_tables(size_count):
    index = jnp.arange(size_count, dtype=jnp.int32)
    angle = (
        2.0
        * math.pi
        / size_count
        * (index[:, None] * index[None, :] % size_count).astype(jnp.float32)
    )
    return (jnp.cos(angle), jnp.sin(angle))


def twiddles(row_count, col_count):
    total = row_count * col_count
    row_index = jnp.arange(row_count, dtype=jnp.int32)
    col_index = jnp.arange(col_count, dtype=jnp.int32)
    angle = (
        2.0
        * math.pi
        / total
        * (row_index[:, None] * col_index[None, :] % total).astype(jnp.float32)
    )
    return (jnp.cos(angle), jnp.sin(angle))


def left_apply(table, blocks):
    return jnp.einsum("ka,cab->ckb", table, blocks, precision=precise)


def right_apply(blocks, table):
    return jnp.einsum("cka,ab->ckb", blocks, table, precision=precise)


def spectrum(signal):
    channels, length = signal.shape
    total = 2 * length
    row_count = 128
    col_count = total // row_count
    padded = jnp.concatenate(
        [signal.astype(jnp.float32), jnp.zeros((channels, length), jnp.float32)], axis=1
    )
    padded = padded.reshape(channels, row_count, col_count)
    cos_rows, sin_rows = dft_tables(row_count)
    cos_cols, sin_cols = dft_tables(col_count)
    cos_twist, sin_twist = twiddles(row_count, col_count)
    first_real = left_apply(cos_rows, padded)
    first_imag = -left_apply(sin_rows, padded)
    turned_real = first_real * cos_twist + first_imag * sin_twist
    turned_imag = first_imag * cos_twist - first_real * sin_twist
    spec_real = right_apply(turned_real, cos_cols) + right_apply(turned_imag, sin_cols)
    spec_imag = right_apply(turned_imag, cos_cols) - right_apply(turned_real, sin_cols)
    return (spec_real, spec_imag)


def signal_of(spec_real, spec_imag, length):
    channels, row_count, col_count = spec_real.shape
    total = row_count * col_count
    cos_rows, sin_rows = dft_tables(row_count)
    cos_cols, sin_cols = dft_tables(col_count)
    cos_twist, sin_twist = twiddles(row_count, col_count)
    back_real = right_apply(spec_real, cos_cols) - right_apply(spec_imag, sin_cols)
    back_imag = right_apply(spec_imag, cos_cols) + right_apply(spec_real, sin_cols)
    turned_real = back_real * cos_twist - back_imag * sin_twist
    turned_imag = back_imag * cos_twist + back_real * sin_twist
    values = left_apply(cos_rows, turned_real) - left_apply(sin_rows, turned_imag)
    return values.reshape(channels, total)[:, :length] / total


def times_plain(left_real, left_imag, right_real, right_imag):
    return (
        left_real * right_real - left_imag * right_imag,
        left_real * right_imag + left_imag * right_real,
    )


def times_conj(left_real, left_imag, right_real, right_imag):
    return (
        left_real * right_real + left_imag * right_imag,
        left_imag * right_real - left_real * right_imag,
    )


def channel_total(values):
    return lax.psum(values, "tp")


def per_device(query, key_proj, value_proj, filter_taps, grad_out):
    length = query.shape[0] * lax.axis_size("ctx")
    width = query.shape[1] * lax.axis_size("tp")
    filter_scale = 1.0 / math.sqrt(length)
    key_cols, value_cols, taps_cols = (
        lax.all_to_all(key_proj.T, "ctx", split_axis=0, concat_axis=1, tiled=True),
        lax.all_to_all(value_proj.T, "ctx", split_axis=0, concat_axis=1, tiled=True),
        lax.all_to_all(filter_taps.T, "ctx", split_axis=0, concat_axis=1, tiled=True),
    )
    mixed_cols = (key_cols.astype(jnp.float32) * value_cols.astype(jnp.float32)).astype(
        jnp.bfloat16
    )
    taps_real, taps_imag = spectrum(taps_cols)
    mixed_real, mixed_imag = spectrum(mixed_cols)
    conv_real, conv_imag = times_plain(mixed_real, mixed_imag, taps_real, taps_imag)
    conv_cols = (filter_scale * signal_of(conv_real, conv_imag, length)).astype(jnp.bfloat16)
    conv_rows = lax.all_to_all(conv_cols, "ctx", split_axis=1, concat_axis=0, tiled=True).T
    conv_float = conv_rows.astype(jnp.float32)
    query_float = query.astype(jnp.float32)
    gated = query_float * conv_float
    upstream = grad_out.astype(jnp.float32)
    square_sum = channel_total(jnp.sum(gated * gated, axis=1))
    inverse_rms = lax.rsqrt(square_sum / width + 1e-05)
    mixer_out = (gated * inverse_rms[:, None]).astype(jnp.bfloat16)
    dots = channel_total(jnp.sum(upstream * gated, axis=1)) / width
    dgated = inverse_rms[:, None] * upstream - (inverse_rms**3 * dots)[:, None] * gated
    dquery = (dgated * conv_float).astype(jnp.bfloat16)
    gconv = (dgated * query_float).astype(jnp.bfloat16)
    grad_cols = lax.all_to_all(gconv.T, "ctx", split_axis=0, concat_axis=1, tiled=True)
    grad_real, grad_imag = spectrum(grad_cols)
    back_real, back_imag = times_conj(grad_real, grad_imag, taps_real, taps_imag)
    dmixed_cols = (filter_scale * signal_of(back_real, back_imag, length)).astype(jnp.bfloat16)
    tap_real, tap_imag = times_conj(grad_real, grad_imag, mixed_real, mixed_imag)
    dtaps_cols = (filter_scale * signal_of(tap_real, tap_imag, length)).astype(jnp.bfloat16)
    dmixed_float = dmixed_cols.astype(jnp.float32)
    dkey_cols = (dmixed_float * value_cols.astype(jnp.float32)).astype(jnp.bfloat16)
    dvalue_cols = (dmixed_float * key_cols.astype(jnp.float32)).astype(jnp.bfloat16)
    dkey_back, dvalue_back, dtaps_back = (
        lax.all_to_all(dkey_cols, "ctx", split_axis=1, concat_axis=0, tiled=True),
        lax.all_to_all(dvalue_cols, "ctx", split_axis=1, concat_axis=0, tiled=True),
        lax.all_to_all(dtaps_cols, "ctx", split_axis=1, concat_axis=0, tiled=True),
    )
    dkey = dkey_back.T
    dvalue = dvalue_back.T
    dtaps = dtaps_back.T
    return (mixer_out, dquery, dkey, dvalue, dtaps)


def solution(mesh):
    in_specs = (P("ctx", "tp"), P("ctx", "tp"), P("ctx", "tp"), P("ctx", "tp"), P("ctx", "tp"))
    out_specs = (P("ctx", "tp"), P("ctx", "tp"), P("ctx", "tp"), P("ctx", "tp"), P("ctx", "tp"))
    return jax.shard_map(
        per_device, mesh=mesh, in_specs=in_specs, out_specs=out_specs, check_vma=False
    )
```

profile of v0, /device:TPU:1, one launch (start us, length us, event | category | flops | bytes accessed | tf_op | source)
XLA Modules:
  0.0 244.5 jit_solution(10890862937073430349)
XLA Ops:
  0.6 1.7 copy.86
  2.3 18.2 %all-to-all-start = ((bf16[64,8,128]{2,1,0:T(8,128)(2,1)}), bf16[64,8,128]{2,1,0:T(8,128)(2,1)S(1)}, u32[]{:S(2)}, u32[]{:S(2)}) async-start(bf16[64,8,128]{2,1,0:T(8,128)(2,1)} %bitcast.1), calls=%async_computation | async-start | bytes 262144 | tf_op jit(solution)/shard_map/all_to_all | solution.py:101
  21.3 16.4 %all-to-all-done = bf16[64,8,128]{2,1,0:T(8,128)(2,1)S(1)} async-done(((bf16[64,8,128]{2,1,0:T(8,128)(2,1)}), bf16[64,8,128]{2,1,0:T(8,128)(2,1)S(1)}, u32[]{:S(2)}, u32[]{:S(2)}) %all-to-all-start) | async-done | bytes 131104 | tf_op jit(solution)/shard_map/all_to_all | solution.py:101
  37.6 4.4 %all-to-all-start.2 = ((bf16[64,8,128]{2,1,0:T(8,128)(2,1)}), bf16[64,8,128]{2,1,0:T(8,128)(2,1)S(1)}, u32[]{:S(2)}, u32[]{:S(2)}) async-start(bf16[64,8,128]{2,1,0:T(8,128)(2,1)} %bitcast.13), calls=%async_computation.2 | async-start | bytes 262144 | tf_op jit(solution)/shard_map/all_to_all | solution.py:103
  44.1 15.2 %all-to-all-done.2 = bf16[64,8,128]{2,1,0:T(8,128)(2,1)S(1)} async-done(((bf16[64,8,128]{2,1,0:T(8,128)(2,1)}), bf16[64,8,128]{2,1,0:T(8,128)(2,1)S(1)}, u32[]{:S(2)}, u32[]{:S(2)}) %all-to-all-start.2) | async-done | bytes 131104 | tf_op jit(solution)/shard_map/all_to_all | solution.py:103
  59.3 4.6 %all-to-all-start.1 = ((bf16[64,8,128]{2,1,0:T(8,128)(2,1)}), bf16[64,8,128]{2,1,0:T(8,128)(2,1)S(1)}, u32[]{:S(2)}, u32[]{:S(2)}) async-start(bf16[64,8,128]{2,1,0:T(8,128)(2,1)} %bitcast.5), calls=%async_computation.1 | async-start | bytes 262144 | tf_op jit(solution)/shard_map/all_to_all | solution.py:102
  65.3 15.7 %all-to-all-done.1 = bf16[64,8,128]{2,1,0:T(8,128)(2,1)S(1)} async-done(((bf16[64,8,128]{2,1,0:T(8,128)(2,1)}), bf16[64,8,128]{2,1,0:T(8,128)(2,1)S(1)}, u32[]{:S(2)}, u32[]{:S(2)}) %all-to-all-start.1) | async-done | bytes 131104 | tf_op jit(solution)/shard_map/all_to_all | solution.py:102
  82.4 1.2 fusion.67
  83.6 1.2 fusion.66
  84.8 1.2 fusion.69
  86.0 1.2 fusion.68
  87.2 1.2 convolution_add_fusion.5
  88.4 1.2 convolution_subtract_fusion.7
  89.6 1.2 convolution_add_fusion.4
  90.8 1.4 multiply_subtract_fusion.3
  93.1 0.9 fusion.108
  94.9 0.9 convolution_add_fusion.3
  98.7 4.6 %all-to-all-start.3 = ((bf16[8,64,128]{2,0,1:T(8,128)(2,1)}), bf16[8,64,128]{2,0,1:T(8,128)(2,1)S(1)}, u32[]{:S(2)}, u32[]{:S(2)}) async-start(bf16[8,64,128]{2,0,1:T(8,128)(2,1)} %fusion.61), calls=%async_computation.3 | async-start | bytes 262144 | tf_op jit(solution)/shard_map/all_to_all | solution.py:112
  104.3 16.2 %all-to-all-done.3 = bf16[8,64,128]{2,0,1:T(8,128)(2,1)S(1)} async-done(((bf16[8,64,128]{2,0,1:T(8,128)(2,1)}), bf16[8,64,128]{2,0,1:T(8,128)(2,1)S(1)}, u32[]{:S(2)}, u32[]{:S(2)}) %all-to-all-start.3) | async-done | bytes 131104 | tf_op jit(solution)/shard_map/all_to_all | solution.py:112
  120.6 20.4 %all-reduce.3 = (f32[128]{0:T(128)S(1)}, f32[128]{0:T(128)S(1)}) all-reduce(f32[128]{0:T(128)S(1)} %get-tuple-element.16, f32[128]{0:T(128)S(1)} %get-tuple-element.15), channel_id=1, replica_groups=mesh['ctx'=64,'tp'=8] {'tp'}, use_global_device_ids=true, to_apply=%region_1.2 | all-reduce | flops 256 | bytes 2048 | tf_op jit(solution)/shard_map/psum | solution.py:93
  141.8 24.6 %all_to_all.122 = bf16[64,8,128]{2,1,0:T(8,128)(2,1)S(1)} all-to-all(bf16[64,8,128]{2,1,0:T(8,128)(2,1)S(1)} %get-tuple-element.29), channel_id=1, replica_groups=mesh['ctx'=64,'tp'=8] {'ctx'}, dimensions={0} | all-to-all | bytes 262144 | tf_op jit(solution)/shard_map/all_to_all | solution.py:124
  167.7 1.2 fusion.71
  168.9 1.2 fusion.70
  170.1 1.2 convolution_add_fusion.2
  171.3 1.3 multiply_add_fusion
  173.5 0.9 fusion.95
  179.2 4.4 %all-to-all-start.7 = ((bf16[8,64,128]{2,0,1:T(8,128)(2,1)}), bf16[8,64,128]{2,0,1:T(8,128)(2,1)S(1)}, u32[]{:S(2)}, u32[]{:S(2)}) async-start(bf16[8,64,128]{2,0,1:T(8,128)(2,1)} %fusion.62), calls=%async_computation.7 | async-start | bytes 262144 | tf_op jit(solution)/shard_map/all_to_all | solution.py:136
  184.5 0.9 fusion.102
  190.1 10.8 %all-to-all-done.7 = bf16[8,64,128]{2,0,1:T(8,128)(2,1)S(1)} async-done(((bf16[8,64,128]{2,0,1:T(8,128)(2,1)}), bf16[8,64,128]{2,0,1:T(8,128)(2,1)S(1)}, u32[]{:S(2)}, u32[]{:S(2)}) %all-to-all-start.7) | async-done | bytes 131104 | tf_op jit(solution)/shard_map/all_to_all | solution.py:136
  200.9 20.8 %all_to_all.123 = bf16[8,64,128]{2,0,1:T(8,128)(2,1)S(1)} all-to-all(bf16[8,64,128]{2,0,1:T(8,128)(2,1)S(1)} %get-tuple-element.27), channel_id=1, replica_groups=mesh['ctx'=64,'tp'=8] {'ctx'}, dimensions={1} | all-to-all | bytes 262144 | tf_op jit(solution)/shard_map/all_to_all | solution.py:135
  221.7 4.6 %all-to-all-start.5 = ((bf16[8,64,128]{2,0,1:T(8,128)(2,1)}), bf16[8,64,128]{2,0,1:T(8,128)(2,1)S(1)}, u32[]{:S(2)}, u32[]{:S(2)}) async-start(bf16[8,64,128]{2,0,1:T(8,128)(2,1)} %get-tuple-element.28), calls=%async_computation.5 | async-start | bytes 262144 | tf_op jit(solution)/shard_map/all_to_all | solution.py:134
  229.5 14.0 %all-to-all-done.5 = bf16[8,64,128]{2,0,1:T(8,128)(2,1)S(1)} async-done(((bf16[8,64,128]{2,0,1:T(8,128)(2,1)}), bf16[8,64,128]{2,0,1:T(8,128)(2,1)S(1)}, u32[]{:S(2)}, u32[]{:S(2)}) %all-to-all-start.5) | async-done | bytes 131104 | tf_op jit(solution)/shard_map/all_to_all | solution.py:134
  (61 shorter events, 28.3 us)
Async XLA Ops:
  2.3 18.2 %copy-start.2 = (bf16[128,512]{1,0:T(8,128)(2,1)S(1)}, bf16[128,512]{1,0:T(8,128)(2,1)}, u32[]{:S(2)}) copy-start(bf16[128,512]{1,0:T(8,128)(2,1)} %param.8) | copy-start | bytes 393220
  2.3 35.3 %all-to-all-start = ((bf16[64,8,128]{2,1,0:T(8,128)(2,1)}), bf16[64,8,128]{2,1,0:T(8,128)(2,1)S(1)}, u32[]{:S(2)}, u32[]{:S(2)}) async-start(bf16[64,8,128]{2,1,0:T(8,128)(2,1)} %bitcast.1), calls=%async_computation | async-start | bytes 262144 | tf_op jit(solution)/shard_map/all_to_all | solution.py:101
  37.6 21.7 %all-to-all-start.2 = ((bf16[64,8,128]{2,1,0:T(8,128)(2,1)}), bf16[64,8,128]{2,1,0:T(8,128)(2,1)S(1)}, u32[]{:S(2)}, u32[]{:S(2)}) async-start(bf16[64,8,128]{2,1,0:T(8,128)(2,1)} %bitcast.13), calls=%async_computation.2 | async-start | bytes 262144 | tf_op jit(solution)/shard_map/all_to_all | solution.py:103
  42.4 0.9 copy-start.3
  59.3 21.7 %all-to-all-start.1 = ((bf16[64,8,128]{2,1,0:T(8,128)(2,1)}), bf16[64,8,128]{2,1,0:T(8,128)(2,1)S(1)}, u32[]{:S(2)}, u32[]{:S(2)}) async-start(bf16[64,8,128]{2,1,0:T(8,128)(2,1)} %bitcast.5), calls=%async_computation.1 | async-start | bytes 262144 | tf_op jit(solution)/shard_map/all_to_all | solution.py:102
  98.6 4.6 %copy-start.4 = (bf16[128,512]{1,0:T(8,128)(2,1)S(1)}, bf16[128,512]{1,0:T(8,128)(2,1)}, u32[]{:S(2)}) copy-start(bf16[128,512]{1,0:T(8,128)(2,1)} %param.5) | copy-start | bytes 393220
  98.7 21.8 %all-to-all-start.3 = ((bf16[8,64,128]{2,0,1:T(8,128)(2,1)}), bf16[8,64,128]{2,0,1:T(8,128)(2,1)S(1)}, u32[]{:S(2)}, u32[]{:S(2)}) async-start(bf16[8,64,128]{2,0,1:T(8,128)(2,1)} %fusion.61), calls=%async_computation.3 | async-start | bytes 262144 | tf_op jit(solution)/shard_map/all_to_all | solution.py:112
  103.3 0.9 copy-start.5
  179.2 21.7 %all-to-all-start.7 = ((bf16[8,64,128]{2,0,1:T(8,128)(2,1)}), bf16[8,64,128]{2,0,1:T(8,128)(2,1)S(1)}, u32[]{:S(2)}, u32[]{:S(2)}) async-start(bf16[8,64,128]{2,0,1:T(8,128)(2,1)} %fusion.62), calls=%async_computation.7 | async-start | bytes 262144 | tf_op jit(solution)/shard_map/all_to_all | solution.py:136
  221.7 4.6 %copy-start.1 = (bf16[128,512]{0,1:T(8,128)(2,1)S(1)}, bf16[128,512]{0,1:T(8,128)(2,1)}, u32[]{:S(2)}) copy-start(bf16[128,512]{0,1:T(8,128)(2,1)} %get-tuple-element.30) | copy-start | bytes 393220
  221.7 21.8 %all-to-all-start.5 = ((bf16[8,64,128]{2,0,1:T(8,128)(2,1)}), bf16[8,64,128]{2,0,1:T(8,128)(2,1)S(1)}, u32[]{:S(2)}, u32[]{:S(2)}) async-start(bf16[8,64,128]{2,0,1:T(8,128)(2,1)} %get-tuple-element.28), calls=%async_computation.5 | async-start | bytes 262144 | tf_op jit(solution)/shard_map/all_to_all | solution.py:134
  226.3 0.9 copy-start
where the time goes:
time: 248 us; the launch traced here: 245 us
  waiting for transfers between devices  88.3 us (36%)
  blocking collectives  65.8 us (27%)
  starting transfers between devices  40.9 us (16%)
  matrix products  34 us (14%)
  local copies, waits for them, and re-layouts  10.6 us (4%)
  other arithmetic  3.55 us (1%)
    dot_general x24, matrix products, right_apply(): return jnp.einsum('cka,ab->ckb', blocks, table, precision=precise)  25.1 us
    all_to_all x1, blocking collectives, per_device(): lax.all_to_all(gconv.T, 'ctx', split_axis=0, concat_axis=1, tiled=True)  24.6 us
    all_to_all x1, blocking collectives, per_device(): lax.all_to_all(dvalue_cols, 'ctx', split_axis=1, concat_axis=0, tiled=True)  20.8 us
    psum x1, blocking collectives, channel_total(): return lax.psum(values, 'tp')  20.4 us
    all_to_all x1, starting transfers between devices, per_device(): lax.all_to_all(key_proj.T, 'ctx', split_axis=0, concat_axis=1, tiled=True)  18.2 us
    all_to_all x1, waiting for transfers between devices, per_device(): lax.all_to_all(key_proj.T, 'ctx', split_axis=0, concat_axis=1, tiled=True)  16.4 us
    all_to_all x1, waiting for transfers between devices, per_device(): lax.all_to_all(conv_cols, 'ctx', split_axis=1, concat_axis=0, tiled=True)  16.2 us
    all_to_all x1, waiting for transfers between devices, per_device(): lax.all_to_all(value_proj.T, 'ctx', split_axis=0, concat_axis=1, tiled=True)  15.7 us
  transfers between devices with their start and end apart: 6, of which 6 were waited for; matrix products, arithmetic and copies ran while one was open for 5% of the time, Pallas kernels for 0%

commit v1 on v0

v1 whole, which is shorter than its diff:
```python
import functools
import math

import jax
import jax.numpy as jnp
import ml_dtypes
import numpy as np
from jax import lax
from jax.experimental import pallas as pl
from jax.experimental.pallas import tpu as pltpu
from jax.sharding import PartitionSpec as P

MESH = pl.DeviceIdType.MESH
F32 = jnp.float32
BF16 = jnp.bfloat16
EPS = 1e-05


def halves(table):
    high = table.astype(ml_dtypes.bfloat16)
    low = (table - high.astype(np.float64)).astype(ml_dtypes.bfloat16)
    return high, low


def tables(blocks, lanes):
    total = blocks * lanes
    i = np.arange(blocks, dtype=np.float64)
    j = np.arange(lanes, dtype=np.float64)
    outer = 2 * np.pi * np.outer(i + 0.25, i) / blocks
    first = np.concatenate([np.cos(outer), -np.sin(outer)], axis=0)
    first_high, first_low = halves(first)
    first_table = np.concatenate([first_high, first_low], axis=1)
    last_high, last_low = halves(np.ascontiguousarray(first.T))
    last_table = np.concatenate([last_high, last_high, last_low], axis=1)
    turn = 2 * np.pi * np.outer(i + 0.25, j) / total
    inner = 2 * np.pi * (np.outer(j, j) % lanes) / lanes
    cos, sin = np.cos(inner), np.sin(inner)
    ahead = np.block([[cos, -sin], [sin, cos]])
    back = np.block([[cos, sin], [-sin, cos]])
    inner_tables = []
    for table in (ahead, back):
        high, low = halves(table)
        inner_tables.append(np.concatenate([high, high, low], axis=0))
    return (
        first_table,
        last_table,
        inner_tables[0],
        inner_tables[1],
        np.cos(turn).astype(np.float32),
        np.sin(turn).astype(np.float32),
    )


def split(values):
    high = values.astype(BF16)
    return high, (values - high.astype(F32)).astype(BF16)


def dot(left, right):
    return jnp.dot(left, right, preferred_element_type=F32)


def kernel(
    n, m, width, scale,
    query_ref, key_ref, value_ref, taps_ref, grad_ref,
    first_ref, last_ref, ahead_ref, back_ref, cos_ref, sin_ref,
    mixer_ref, dquery_ref, dkey_ref, dvalue_ref, dtaps_ref,
    send1, recv1, send2, recv2, send3, recv3, send4, recv4,
    stat_out, stat_in, shuffle, query_t, grad_t, conv_t, taps_spec, mixed_spec,
    send_sem, recv_sem,
):
    me = lax.axis_index("ctx")
    mine = lax.axis_index("tp")
    rows, cols = query_ref.shape
    group = cols // n
    chips = n // 4

    barrier = pltpu.get_barrier_semaphore()

    def greet_ctx(step, carry):
        peer = lax.rem(me + step, n)
        pl.semaphore_signal(barrier, inc=1, device_id=(peer, mine), device_id_type=MESH)
        return carry

    def greet_tp(step, carry):
        peer = lax.rem(mine + step, m)
        pl.semaphore_signal(barrier, inc=1, device_id=(me, peer), device_id_type=MESH)
        return carry

    lax.fori_loop(1, n, greet_ctx, 0)
    lax.fori_loop(1, m, greet_tp, 0)

    def exchange(phase, source, target):
        side = me // (2 * chips)
        place = lax.rem(me // 2, chips)
        core = lax.rem(me, 2)

        def start(step, carry):
            quarter = lax.rem(step, 4)
            turn = step // 4
            half = lax.rem(turn, 2)
            far = jnp.where(half == 0, chips // 2 + turn // 2, chips // 2 - (turn + 1) // 2)
            flip = quarter // 2
            swap = lax.rem(quarter, 2)
            peer = (
                lax.rem(side + flip, 2) * (2 * chips)
                + lax.rem(place + far, chips) * 2
                + lax.rem(core + swap, 2)
            )
            pltpu.make_async_remote_copy(
                src_ref=source.at[peer],
                dst_ref=target.at[me],
                send_sem=send_sem.at[phase],
                recv_sem=recv_sem.at[phase],
                device_id=(peer, mine),
                device_id_type=MESH,
            ).start()
            return carry

        lax.fori_loop(0, n - 4, start, 0)
        lax.fori_loop(n - 3, n, start, 0)
        target[me] = source[me]

    def arrived(phase, source, target):
        pltpu.make_async_copy(
            source.at[pl.ds(0, n - 1)], target.at[pl.ds(0, n - 1)], recv_sem.at[phase]
        ).wait()

    def sent(phase, source, target):
        pltpu.make_async_copy(
            source.at[pl.ds(0, n - 1)], target.at[pl.ds(0, n - 1)], send_sem.at[phase]
        ).wait()

    def stage_first(blocks):
        shuffle[...] = blocks.astype(F32).reshape(n * group, rows)
        columns = jnp.concatenate(
            [shuffle[pl.ds(c, n, stride=group), :].astype(BF16) for c in range(group)], axis=1
        )
        outer = dot(first_ref[...], jnp.concatenate([columns, columns], axis=0))
        cos, sin = cos_ref[...], sin_ref[...]
        turned = []
        for c in range(group):
            real = outer[:n, c * rows : (c + 1) * rows]
            imag = outer[n:, c * rows : (c + 1) * rows]
            turned.append(
                jnp.concatenate([real * cos + imag * sin, imag * cos - real * sin], axis=1)
            )
        high, low = split(jnp.concatenate(turned, axis=0))
        return dot(jnp.concatenate([high, low, high], axis=1), ahead_ref[...])

    def stage_last(real, imag):
        high, low = split(jnp.concatenate([real, imag], axis=1))
        inner = dot(jnp.concatenate([high, low, high], axis=1), back_ref[...])
        cos, sin = cos_ref[...], sin_ref[...]
        turned = []
        for c in range(group):
            real = inner[c * n : (c + 1) * n, :rows]
            imag = inner[c * n : (c + 1) * n, rows:]
            turned.append(
                jnp.concatenate([real * cos - imag * sin, real * sin + imag * cos], axis=0)
            )
        high, low = split(jnp.concatenate(turned, axis=1))
        outer = dot(last_ref[...], jnp.concatenate([high, low, high], axis=0))
        for c in range(group):
            shuffle[pl.ds(c, n, stride=group), :] = outer[:, c * rows : (c + 1) * rows] * scale
        return shuffle[...].reshape(n, group, rows)

    mixed = (key_ref[...].astype(F32) * value_ref[...].astype(F32)).astype(BF16).astype(F32)
    send1[:, :group, :] = mixed.T.reshape(n, group, rows).astype(BF16)
    send1[:, group:, :] = taps_ref[...].astype(F32).T.reshape(n, group, rows).astype(BF16)
    pl.semaphore_wait(barrier, n + m - 2)
    exchange(0, send1, recv1)
    query_t[...] = query_ref[...].astype(F32).T
    grad_t[...] = grad_ref[...].astype(F32).T
    stat_out[...] = jnp.zeros_like(stat_out)
    arrived(0, send1, recv1)

    mixed_spec[...] = stage_first(recv1[:, :group, :])
    taps_spec[...] = stage_first(recv1[:, group:, :])
    mixed_real, mixed_imag = mixed_spec[:, :rows], mixed_spec[:, rows:]
    taps_real, taps_imag = taps_spec[:, :rows], taps_spec[:, rows:]
    send2[...] = stage_last(
        mixed_real * taps_real - mixed_imag * taps_imag,
        mixed_real * taps_imag + mixed_imag * taps_real,
    ).astype(BF16)
    exchange(1, send2, recv2)
    arrived(1, send2, recv2)

    conv_t[...] = recv2[...].astype(F32).reshape(cols, rows)
    gated = query_t[...] * conv_t[...]
    stat_out[0:1, :] = jnp.sum(gated * gated, axis=0, keepdims=True)
    stat_out[1:2, :] = jnp.sum(grad_t[...] * gated, axis=0, keepdims=True)

    def send_stats(step, carry):
        peer = lax.rem(mine + step, m)
        pltpu.make_async_remote_copy(
            src_ref=stat_out,
            dst_ref=stat_in.at[mine],
            send_sem=send_sem.at[4],
            recv_sem=recv_sem.at[4],
            device_id=(me, peer),
            device_id_type=MESH,
        ).start()
        return carry

    lax.fori_loop(1, m, send_stats, 0)
    stat_in[mine] = stat_out[...]
    pltpu.make_async_copy(
        stat_in.at[pl.ds(0, m - 1)], stat_in.at[pl.ds(0, m - 1)], recv_sem.at[4]
    ).wait()
    totals = jnp.sum(stat_in[...], axis=0)
    inverse_rms = lax.rsqrt(totals[0:1, :] / width + EPS)
    dots = totals[1:2, :] / width
    weight = inverse_rms * inverse_rms * inverse_rms * dots

    gated = query_t[...] * conv_t[...]
    dgated = inverse_rms * grad_t[...] - weight * gated
    send3[...] = (dgated * query_t[...]).astype(BF16).reshape(n, group, rows)
    exchange(2, send3, recv3)
    mixer_ref[...] = (gated * inverse_rms).T.astype(BF16)
    dquery_ref[...] = (dgated * conv_t[...]).T.astype(BF16)
    arrived(2, send3, recv3)

    grads = stage_first(recv3[...])
    grads_real, grads_imag = grads[:, :rows], grads[:, rows:]
    taps_real, taps_imag = taps_spec[:, :rows], taps_spec[:, rows:]
    send4[:, :group, :] = stage_last(
        grads_real * taps_real + grads_imag * taps_imag,
        grads_imag * taps_real - grads_real * taps_imag,
    ).astype(BF16)
    mixed_real, mixed_imag = mixed_spec[:, :rows], mixed_spec[:, rows:]
    send4[:, group:, :] = stage_last(
        grads_real * mixed_real + grads_imag * mixed_imag,
        grads_imag * mixed_real - grads_real * mixed_imag,
    ).astype(BF16)
    exchange(3, send4, recv4)
    arrived(3, send4, recv4)

    dmixed = recv4[:, :group, :].astype(F32).reshape(cols, rows).T
    dkey_ref[...] = (dmixed * value_ref[...].astype(F32)).astype(BF16)
    dvalue_ref[...] = (dmixed * key_ref[...].astype(F32)).astype(BF16)
    dtaps_ref[...] = recv4[:, group:, :].astype(F32).reshape(cols, rows).T.astype(BF16)

    sent(0, send1, recv1)
    sent(1, send2, recv2)
    sent(2, send3, recv3)
    sent(3, send4, recv4)
    pltpu.make_async_copy(
        stat_in.at[pl.ds(0, m - 1)], stat_in.at[pl.ds(0, m - 1)], send_sem.at[4]
    ).wait()


def per_device(n, m, query, key_proj, value_proj, filter_taps, grad_out):
    rows, cols = query.shape
    group = cols // n
    length = rows * n
    consts = [jnp.asarray(table) for table in tables(n, rows)]
    vmem = pl.BlockSpec(memory_space=pltpu.VMEM)
    one = pltpu.VMEM((n, group, rows), BF16)
    two = pltpu.VMEM((n, 2 * group, rows), BF16)
    wide = pltpu.VMEM((cols, rows), F32)
    return pl.pallas_call(
        functools.partial(kernel, n, m, cols * m, 1.0 / (math.sqrt(length) * length)),
        out_shape=[jax.ShapeDtypeStruct((rows, cols), BF16)] * 5,
        in_specs=[vmem] * 11,
        out_specs=[vmem] * 5,
        scratch_shapes=[
            two, two, one, one, one, one, two, two,
            pltpu.VMEM((8, rows), F32),
            pltpu.VMEM((m, 8, rows), F32),
            pltpu.VMEM((n * group, rows), F32),
            wide, wide, wide,
            pltpu.VMEM((n * group, 2 * rows), F32),
            pltpu.VMEM((n * group, 2 * rows), F32),
            pltpu.SemaphoreType.DMA((5,)),
            pltpu.SemaphoreType.DMA((5,)),
        ],
        compiler_params=pltpu.CompilerParams(
            collective_id=0, has_side_effects=True, vmem_limit_bytes=48 * 1024 * 1024
        ),
    )(query, key_proj, value_proj, filter_taps, grad_out, *consts)


def solution(mesh):
    spec = P("ctx", "tp")
    return jax.shard_map(
        functools.partial(per_device, mesh.shape["ctx"], mesh.shape["tp"]),
        mesh=mesh,
        in_specs=(spec,) * 5,
        out_specs=(spec,) * 5,
        check_vma=False,
    )
```

time: 248 us -> 89.4 us (0.36); the launches traced: 245 us -> 88.9 us
  waiting for transfers between devices: 88.3 us -> 0 us
  Pallas kernels: 0 us -> 75.4 us
  blocking collectives: 65.8 us -> 0 us
  starting transfers between devices: 40.9 us -> 0 us
  matrix products: 34 us -> 0 us
  other arithmetic: 3.55 us -> 0 us
    all_to_all x6 -> x0, waiting for transfers between devices: 88.3 us -> none  [the longest x1 16.4 us: per_device(): lax.all_to_all(key_proj.T, 'ctx', split_axis=0, concat_axis=1, tiled=True)]
    pallas_call x0 -> x1, Pallas kernels: none -> 75.4 us  [per_device(): pl.pallas_call(functools.partial(kernel, n, m, cols * m, 1.0 / (math.sqrt...]
    all_to_all x2 -> x0, blocking collectives: 45.5 us -> none  [the longest x1 24.6 us: per_device(): lax.all_to_all(gconv.T, 'ctx', split_axis=0, concat_axis=1, tiled=True)]
    all_to_all x6 -> x0, starting transfers between devices: 40.9 us -> none  [the longest x1 18.2 us: per_device(): lax.all_to_all(key_proj.T, 'ctx', split_axis=0, concat_axis=1, tiled=True)]
    dot_general x36 -> x0, matrix products: 34 us -> none  [the longest x24 25.1 us: right_apply(): return jnp.einsum('cka,ab->ckb', blocks, table, precision=precise)]
    psum x1 -> x0, blocking collectives: 20.4 us -> none  [channel_total(): return lax.psum(values, 'tp')]
    unnamed x28 -> x27, local copies, waits for them, and re-layouts: 9.88 us -> 12.9 us
    all_to_all x4 -> x0, other arithmetic: 2.9 us -> none  [the longest x1 0.82 us: per_device(): lax.all_to_all(gconv.T, 'ctx', split_axis=0, concat_axis=1, tiled=True)]
  transfers between devices with their start and end apart: 6 -> 0, of which waited for: 6 -> 0; matrix products, arithmetic and copies ran while one was open for 5% -> 0% of each run, Pallas kernels for 0% -> 0%
where the time goes in v1:
time: 89.4 us; the launch traced here: 88.9 us
  Pallas kernels  75.4 us (84%)
  local copies, waits for them, and re-layouts  12.9 us (14%)
    pallas_call x1, Pallas kernels, per_device(): pl.pallas_call(functools.partial(kernel, n, m, cols * m, 1.0 / (math.sqrt...  75.4 us
    unnamed x27, local copies, waits for them, and re-layouts  12.9 us

profile of v1, /device:TPU:1, one launch (start us, length us, event | category | flops | bytes accessed | tf_op | source)
XLA Modules:
  0.0 88.9 jit_solution(4566253260054380221)
XLA Ops:
  0.6 0.0 copy-start
  0.6 1.0 %copy-done = bf16[768,256]{1,0:T(8,128)(2,1)S(1)} copy-done((bf16[768,256]{1,0:T(8,128)(2,1)S(1)}, bf16[768,256]{1,0:T(8,128)(2,1)}, u32[]{:S(2)}) %copy-start) | copy-done | bytes 393240
  1.6 0.0 copy-start.1
  1.6 1.0 %copy-done.1 = bf16[768,256]{1,0:T(8,128)(2,1)S(1)} copy-done((bf16[768,256]{1,0:T(8,128)(2,1)S(1)}, bf16[768,256]{1,0:T(8,128)(2,1)}, u32[]{:S(2)}) %copy-start.1) | copy-done | bytes 393240
  2.6 0.0 copy-start.2
  2.6 0.9 %copy-done.2 = bf16[128,512]{1,0:T(8,128)(2,1)S(1)} copy-done((bf16[128,512]{1,0:T(8,128)(2,1)S(1)}, bf16[128,512]{1,0:T(8,128)(2,1)}, u32[]{:S(2)}) %copy-start.2) | copy-done | bytes 131096
  3.5 0.0 copy-start.3
  3.5 0.9 %copy-done.3 = bf16[128,512]{1,0:T(8,128)(2,1)S(1)} copy-done((bf16[128,512]{1,0:T(8,128)(2,1)S(1)}, bf16[128,512]{1,0:T(8,128)(2,1)}, u32[]{:S(2)}) %copy-start.3) | copy-done | bytes 131096
  4.4 0.0 copy-start.4
  4.4 0.9 %copy-done.4 = bf16[128,512]{1,0:T(8,128)(2,1)S(1)} copy-done((bf16[128,512]{1,0:T(8,128)(2,1)S(1)}, bf16[128,512]{1,0:T(8,128)(2,1)}, u32[]{:S(2)}) %copy-start.4) | copy-done | bytes 131096
  5.3 0.0 copy-start.5
  5.3 0.9 %copy-done.5 = bf16[128,512]{1,0:T(8,128)(2,1)S(1)} copy-done((bf16[128,512]{1,0:T(8,128)(2,1)S(1)}, bf16[128,512]{1,0:T(8,128)(2,1)}, u32[]{:S(2)}) %copy-start.5) | copy-done | bytes 131096
  6.2 0.0 copy-start.6
  6.2 0.9 %copy-done.6 = bf16[128,512]{1,0:T(8,128)(2,1)S(1)} copy-done((bf16[128,512]{1,0:T(8,128)(2,1)S(1)}, bf16[128,512]{1,0:T(8,128)(2,1)}, u32[]{:S(2)}) %copy-start.6) | copy-done | bytes 131096
  7.2 0.0 copy-start.7
  7.2 0.8 copy-done.7
  8.0 0.0 copy-start.8
  8.0 0.8 copy-done.8
  8.7 0.0 copy-start.9
  8.7 0.8 copy-done.9
  9.5 0.0 copy-start.10
  9.5 0.8 copy-done.10
  10.2 75.4 %shard_map.146 = (bf16[128,512]{1,0:T(8,128)(2,1)S(1)}, bf16[128,512]{1,0:T(8,128)(2,1)S(1)}, bf16[128,512]{1,0:T(8,128)(2,1)S(1)}, bf16[128,512]{1,0:T(8,128)(2,1)S(1)}, bf16[128,512]{1,0:T(8,128)(2,1)S(1)}) custom-call(bf16[128,512]{1,0:T(8,128)(2,1)S(1)} %copy-done.2, bf16[128,512]{1,0:T(8,128)(2,1)S(1)} %copy-done.3, bf16[128,512]{1,0:T(8,128)(2,1)S(1)} %copy-done.4, ...), custom_call_target="tpu_custom_call" | custom-call | tf_op jit(solution)/shard_map/pallas_call | solution.py:262
  85.6 0.7 copy.21
  86.3 0.7 copy.22
  86.9 0.7 copy.23
  87.6 0.7 copy.24
  88.2 0.7 copy.25
Async XLA Ops:
  0.6 1.0 %copy-start = (bf16[768,256]{1,0:T(8,128)(2,1)S(1)}, bf16[768,256]{1,0:T(8,128)(2,1)}, u32[]{:S(2)}) copy-start(bf16[768,256]{1,0:T(8,128)(2,1)} %constant.15.clone.back_ref) | copy-start | bytes 1179652
  1.6 1.0 %copy-start.1 = (bf16[768,256]{1,0:T(8,128)(2,1)S(1)}, bf16[768,256]{1,0:T(8,128)(2,1)}, u32[]{:S(2)}) copy-start(bf16[768,256]{1,0:T(8,128)(2,1)} %constant.14.clone.ahead_ref) | copy-start | bytes 1179652
  2.6 0.9 %copy-start.2 = (bf16[128,512]{1,0:T(8,128)(2,1)S(1)}, bf16[128,512]{1,0:T(8,128)(2,1)}, u32[]{:S(2)}) copy-start(bf16[128,512]{1,0:T(8,128)(2,1)} %query_ref.1) | copy-start | bytes 393220
  3.5 0.9 %copy-start.3 = (bf16[128,512]{1,0:T(8,128)(2,1)S(1)}, bf16[128,512]{1,0:T(8,128)(2,1)}, u32[]{:S(2)}) copy-start(bf16[128,512]{1,0:T(8,128)(2,1)} %key_ref.1) | copy-start | bytes 393220
  4.4 0.9 %copy-start.4 = (bf16[128,512]{1,0:T(8,128)(2,1)S(1)}, bf16[128,512]{1,0:T(8,128)(2,1)}, u32[]{:S(2)}) copy-start(bf16[128,512]{1,0:T(8,128)(2,1)} %value_ref.1) | copy-start | bytes 393220
  5.3 0.9 %copy-start.5 = (bf16[128,512]{1,0:T(8,128)(2,1)S(1)}, bf16[128,512]{1,0:T(8,128)(2,1)}, u32[]{:S(2)}) copy-start(bf16[128,512]{1,0:T(8,128)(2,1)} %taps_ref.1) | copy-start | bytes 393220
  6.2 0.9 %copy-start.6 = (bf16[128,512]{1,0:T(8,128)(2,1)S(1)}, bf16[128,512]{1,0:T(8,128)(2,1)}, u32[]{:S(2)}) copy-start(bf16[128,512]{1,0:T(8,128)(2,1)} %grad_ref.1) | copy-start | bytes 393220
  7.2 0.8 copy-start.7
  8.0 0.8 copy-start.8
  8.7 0.8 copy-start.9
  9.5 0.8 copy-start.10

commit v2 on v1

--- a/solution.py
+++ b/solution.py
@@ -14,6 +14,7 @@
 F32 = jnp.float32
 BF16 = jnp.bfloat16
 EPS = 1e-05
+VMEM_BYTES = 63 * 1024 * 1024
 
 
 def halves(table):
@@ -62,13 +63,34 @@
 
 def kernel(
     n, m, width, scale,
+    query_in, key_in, value_in, taps_in, grad_in,
+    first_in, last_in, ahead_in, back_in, cos_in, sin_in,
+    mixer_out, dquery_out, dkey_out, dvalue_out, dtaps_out,
+    mixer_ref, dquery_ref, dkey_ref, dvalue_ref, dtaps_ref,
     query_ref, key_ref, value_ref, taps_ref, grad_ref,
     first_ref, last_ref, ahead_ref, back_ref, cos_ref, sin_ref,
-    mixer_ref, dquery_ref, dkey_ref, dvalue_ref, dtaps_ref,
-    send1, recv1, send2, recv2, send3, recv3, send4, recv4,
+    send1, recv1, send2, recv2, send3, recv3, send4, recv4, send5, recv5,
     stat_out, stat_in, shuffle, query_t, grad_t, conv_t, taps_spec, mixed_spec,
-    send_sem, recv_sem,
+    send_sem, recv_sem, load_sem, store_sem,
 ):
+    loads = [
+        pltpu.make_async_copy(source, target, load_sem.at[number])
+        for number, (source, target) in enumerate([
+            (key_in, key_ref), (value_in, value_ref), (taps_in, taps_ref),
+            (query_in, query_ref), (grad_in, grad_ref), (first_in, first_ref),
+            (ahead_in, ahead_ref), (back_in, back_ref), (last_in, last_ref),
+            (cos_in, cos_ref), (sin_in, sin_ref),
+        ])
+    ]
+    for load in loads:
+        load.start()
+    mixer_store, dquery_store, dkey_store, dvalue_store, dtaps_store = stores = [
+        pltpu.make_async_copy(source, target, store_sem.at[number])
+        for number, (source, target) in enumerate([
+            (mixer_ref, mixer_out), (dquery_ref, dquery_out), (dkey_ref, dkey_out),
+            (dvalue_ref, dvalue_out), (dtaps_ref, dtaps_out),
+        ])
+    ]
     me = lax.axis_index("ctx")
     mine = lax.axis_index("tp")
     rows, cols = query_ref.shape
@@ -77,36 +99,44 @@
 
     barrier = pltpu.get_barrier_semaphore()
 
-    def greet_ctx(step, carry):
-        peer = lax.rem(me + step, n)
+    side = me // (2 * chips)
+    place = lax.rem(me // 2, chips)
+    core = lax.rem(me, 2)
+
+    def partner(step):
+        turn = step // 4
+        half = lax.rem(turn, 2)
+        far = jnp.where(half == 0, chips // 2 + turn // 2, chips // 2 - (turn + 1) // 2)
+        far = jnp.where(core == 0, far, chips - far)
+        flip = lax.rem(step, 4) // 2
+        swap = lax.rem(step, 2)
+        return (
+            lax.rem(side + flip, 2) * (2 * chips)
+            + lax.rem(place + far, chips) * 2
+            + lax.rem(core + swap, 2)
+        )
+
+    def for_partners(body):
+        def step(number, carry):
+            body(partner(number))
+            return carry
+
+        lax.fori_loop(0, n - 4, step, 0)
+        lax.fori_loop(n - 3, n, step, 0)
+
+    def greet_ctx(peer):
         pl.semaphore_signal(barrier, inc=1, device_id=(peer, mine), device_id_type=MESH)
-        return carry
 
     def greet_tp(step, carry):
         peer = lax.rem(mine + step, m)
         pl.semaphore_signal(barrier, inc=1, device_id=(me, peer), device_id_type=MESH)
         return carry
 
-    lax.fori_loop(1, n, greet_ctx, 0)
+    for_partners(greet_ctx)
     lax.fori_loop(1, m, greet_tp, 0)
 
     def exchange(phase, source, target):
-        side = me // (2 * chips)
-        place = lax.rem(me // 2, chips)
-        core = lax.rem(me, 2)
-
-        def start(step, carry):
-            quarter = lax.rem(step, 4)
-            turn = step // 4
-            half = lax.rem(turn, 2)
-            far = jnp.where(half == 0, chips // 2 + turn // 2, chips // 2 - (turn + 1) // 2)
-            flip = quarter // 2
-            swap = lax.rem(quarter, 2)
-            peer = (
-                lax.rem(side + flip, 2) * (2 * chips)
-                + lax.rem(place + far, chips) * 2
-                + lax.rem(core + swap, 2)
-            )
+        def start(peer):
             pltpu.make_async_remote_copy(
                 src_ref=source.at[peer],
                 dst_ref=target.at[me],
@@ -115,10 +145,8 @@
                 device_id=(peer, mine),
                 device_id_type=MESH,
             ).start()
-            return carry
-
-        lax.fori_loop(0, n - 4, start, 0)
-        lax.fori_loop(n - 3, n, start, 0)
+
+        for_partners(start)
         target[me] = source[me]
 
     def arrived(phase, source, target):
@@ -165,11 +193,15 @@
             shuffle[pl.ds(c, n, stride=group), :] = outer[:, c * rows : (c + 1) * rows] * scale
         return shuffle[...].reshape(n, group, rows)
 
+    for load in loads[:3]:
+        load.wait()
     mixed = (key_ref[...].astype(F32) * value_ref[...].astype(F32)).astype(BF16).astype(F32)
     send1[:, :group, :] = mixed.T.reshape(n, group, rows).astype(BF16)
     send1[:, group:, :] = taps_ref[...].astype(F32).T.reshape(n, group, rows).astype(BF16)
     pl.semaphore_wait(barrier, n + m - 2)
     exchange(0, send1, recv1)
+    for load in loads[3:]:
+        load.wait()
     query_t[...] = query_ref[...].astype(F32).T
     grad_t[...] = grad_ref[...].astype(F32).T
     stat_out[...] = jnp.zeros_like(stat_out)
@@ -196,8 +228,8 @@
         pltpu.make_async_remote_copy(
             src_ref=stat_out,
             dst_ref=stat_in.at[mine],
-            send_sem=send_sem.at[4],
-            recv_sem=recv_sem.at[4],
+            send_sem=send_sem.at[5],
+            recv_sem=recv_sem.at[5],
             device_id=(me, peer),
             device_id_type=MESH,
         ).start()
@@ -206,7 +238,7 @@
     lax.fori_loop(1, m, send_stats, 0)
     stat_in[mine] = stat_out[...]
     pltpu.make_async_copy(
-        stat_in.at[pl.ds(0, m - 1)], stat_in.at[pl.ds(0, m - 1)], recv_sem.at[4]
+        stat_in.at[pl.ds(0, m - 1)], stat_in.at[pl.ds(0, m - 1)], recv_sem.at[5]
     ).wait()
     totals = jnp.sum(stat_in[...], axis=0)
     inverse_rms = lax.rsqrt(totals[0:1, :] / width + EPS)
@@ -219,35 +251,62 @@
     exchange(2, send3, recv3)
     mixer_ref[...] = (gated * inverse_rms).T.astype(BF16)
     dquery_ref[...] = (dgated * conv_t[...]).T.astype(BF16)
+    mixer_store.start()
+    dquery_store.start()
     arrived(2, send3, recv3)
 
     grads = stage_first(recv3[...])
     grads_real, grads_imag = grads[:, :rows], grads[:, rows:]
     taps_real, taps_imag = taps_spec[:, :rows], taps_spec[:, rows:]
-    send4[:, :group, :] = stage_last(
+    send4[...] = stage_last(
         grads_real * taps_real + grads_imag * taps_imag,
         grads_imag * taps_real - grads_real * taps_imag,
     ).astype(BF16)
+    exchange(3, send4, recv4)
     mixed_real, mixed_imag = mixed_spec[:, :rows], mixed_spec[:, rows:]
-    send4[:, group:, :] = stage_last(
+    send5[...] = stage_last(
         grads_real * mixed_real + grads_imag * mixed_imag,
         grads_imag * mixed_real - grads_real * mixed_imag,
     ).astype(BF16)
-    exchange(3, send4, recv4)
+    exchange(4, send5, recv5)
     arrived(3, send4, recv4)
 
-    dmixed = recv4[:, :group, :].astype(F32).reshape(cols, rows).T
+    dmixed = recv4[...].astype(F32).reshape(cols, rows).T
     dkey_ref[...] = (dmixed * value_ref[...].astype(F32)).astype(BF16)
     dvalue_ref[...] = (dmixed * key_ref[...].astype(F32)).astype(BF16)
-    dtaps_ref[...] = recv4[:, group:, :].astype(F32).reshape(cols, rows).T.astype(BF16)
+    dkey_store.start()
+    dvalue_store.start()
+    arrived(4, send5, recv5)
+    dtaps_ref[...] = recv5[...].astype(F32).reshape(cols, rows).T.astype(BF16)
+    dtaps_store.start()
 
     sent(0, send1, recv1)
     sent(1, send2, recv2)
     sent(2, send3, recv3)
     sent(3, send4, recv4)
+    sent(4, send5, recv5)
     pltpu.make_async_copy(
-        stat_in.at[pl.ds(0, m - 1)], stat_in.at[pl.ds(0, m - 1)], send_sem.at[4]
+        stat_in.at[pl.ds(0, m - 1)], stat_in.at[pl.ds(0, m - 1)], send_sem.at[5]
     ).wait()
+    for store in stores:
+        store.wait()
+
+
+def store_kernel(*refs):
+    sources, targets, middles, load_sem, store_sem = refs[:5], refs[5:10], refs[10:15], *refs[15:]
+    loads = [
+        pltpu.make_async_copy(sources[k], middles[k], load_sem.at[k]) for k in range(len(sources))
+    ]
+    stores = [
+        pltpu.make_async_copy(middles[k], targets[k], store_sem.at[k]) for k in range(len(sources))
+    ]
+    for load in loads:
+        load.start()
+    for load, store in zip(loads, stores, strict=True):
+        load.wait()
+        store.start()
+    for store in stores:
+        store.wait()
 
 
 def per_device(n, m, query, key_proj, value_proj, filter_taps, grad_out):
@@ -255,30 +314,45 @@
     group = cols // n
     length = rows * n
     consts = [jnp.asarray(table) for table in tables(n, rows)]
-    vmem = pl.BlockSpec(memory_space=pltpu.VMEM)
+    where = pl.BlockSpec(memory_space=pl.ANY)
     one = pltpu.VMEM((n, group, rows), BF16)
     two = pltpu.VMEM((n, 2 * group, rows), BF16)
     wide = pltpu.VMEM((cols, rows), F32)
-    return pl.pallas_call(
+    local = pltpu.VMEM((rows, cols), BF16)
+    shapes = [jax.ShapeDtypeStruct((rows, cols), BF16)] * 5
+    results = pl.pallas_call(
         functools.partial(kernel, n, m, cols * m, 1.0 / (math.sqrt(length) * length)),
-        out_shape=[jax.ShapeDtypeStruct((rows, cols), BF16)] * 5,
-        in_specs=[vmem] * 11,
-        out_specs=[vmem] * 5,
+        out_shape=shapes,
+        in_specs=[where] * 11,
+        out_specs=[where] * 5,
         scratch_shapes=[
-            two, two, one, one, one, one, two, two,
+            local, local, local, local, local,
+            local, local, local, local, local,
+            *[pltpu.VMEM(table.shape, table.dtype) for table in consts],
+            two, two, one, one, one, one, one, one, one, one,
             pltpu.VMEM((8, rows), F32),
             pltpu.VMEM((m, 8, rows), F32),
             pltpu.VMEM((n * group, rows), F32),
             wide, wide, wide,
             pltpu.VMEM((n * group, 2 * rows), F32),
             pltpu.VMEM((n * group, 2 * rows), F32),
-            pltpu.SemaphoreType.DMA((5,)),
+            pltpu.SemaphoreType.DMA((6,)),
+            pltpu.SemaphoreType.DMA((6,)),
+            pltpu.SemaphoreType.DMA((11,)),
             pltpu.SemaphoreType.DMA((5,)),
         ],
         compiler_params=pltpu.CompilerParams(
-            collective_id=0, has_side_effects=True, vmem_limit_bytes=48 * 1024 * 1024
+            collective_id=0, has_side_effects=True, vmem_limit_bytes=VMEM_BYTES
         ),
     )(query, key_proj, value_proj, filter_taps, grad_out, *consts)
+    return pl.pallas_call(
+        store_kernel,
+        out_shape=shapes,
+        in_specs=[where] * 5,
+        out_specs=[where] * 5,
+        scratch_shapes=[local] * 5 + [pltpu.SemaphoreType.DMA((5,))] * 2,
+        compiler_params=pltpu.CompilerParams(vmem_limit_bytes=VMEM_BYTES),
+    )(*results)
 
 
 def solution(mesh):

time: 89.4 us -> 78.5 us (0.88)
  local copies, waits for them, and re-layouts: 12.9 us -> 0 us
  Pallas kernels: 75.4 us -> 77.7 us
    unnamed x27 -> x0, local copies, waits for them, and re-layouts: 12.9 us -> none
    pallas_call x0 -> x1, Pallas kernels: none -> 1.91 us  [per_device(): pl.pallas_call(store_kernel, out_shape=shapes, in_specs=[where] * 5, out_...]
where the time goes in v2:
time: 78.5 us; the launch traced here: 78.4 us
  Pallas kernels  77.7 us (99%)
    pallas_call x1, Pallas kernels, per_device(): pl.pallas_call(functools.partial(kernel, n, m, cols * m, 1.0 / (math.sqrt...  75.8 us
    pallas_call x1, Pallas kernels, per_device(): pl.pallas_call(store_kernel, out_shape=shapes, in_specs=[where] * 5, out_...  1.91 us

profile of v2, /device:TPU:1, one launch (start us, length us, event | category | flops | bytes accessed | tf_op | source)
XLA Modules:
  0.0 78.4 jit_solution(10592440666834097275)
XLA Ops:
  0.6 75.8 %shard_map.146 = (bf16[128,512]{1,0:T(8,128)(2,1)}, bf16[128,512]{1,0:T(8,128)(2,1)}, bf16[128,512]{1,0:T(8,128)(2,1)}, bf16[128,512]{1,0:T(8,128)(2,1)}, bf16[128,512]{1,0:T(8,128)(2,1)}) custom-call(bf16[128,512]{1,0:T(8,128)(2,1)} %query_in.1, bf16[128,512]{1,0:T(8,128)(2,1)} %key_in.1, bf16[128,512]{1,0:T(8,128)(2,1)} %value_in.1, ...), custom_call_target="tpu_custom_call" | custom-call | tf_op jit(solution)/shard_map/pallas_call | solution.py:323
  76.5 1.9 %shard_map.147 = (bf16[128,512]{1,0:T(8,128)(2,1)}, bf16[128,512]{1,0:T(8,128)(2,1)}, bf16[128,512]{1,0:T(8,128)(2,1)}, bf16[128,512]{1,0:T(8,128)(2,1)}, bf16[128,512]{1,0:T(8,128)(2,1)}) custom-call(bf16[128,512]{1,0:T(8,128)(2,1)} %get-tuple-element.10.refs_0_, bf16[128,512]{1,0:T(8,128)(2,1)} %get-tuple-element.11.refs_1_, ...), custom_call_target="tpu_custom_call" | custom-call | tf_op jit(solution)/shard_map/pallas_call | solution.py:348

commit v3 on v2

--- a/solution.py
+++ b/solution.py
@@ -14,6 +14,8 @@
 F32 = jnp.float32
 BF16 = jnp.bfloat16
 EPS = 1e-05
+AHEAD = 4
+STRIDE = 2
 VMEM_BYTES = 63 * 1024 * 1024
 
 
@@ -65,13 +67,12 @@
     n, m, width, scale,
     query_in, key_in, value_in, taps_in, grad_in,
     first_in, last_in, ahead_in, back_in, cos_in, sin_in,
-    mixer_out, dquery_out, dkey_out, dvalue_out, dtaps_out,
     mixer_ref, dquery_ref, dkey_ref, dvalue_ref, dtaps_ref,
     query_ref, key_ref, value_ref, taps_ref, grad_ref,
     first_ref, last_ref, ahead_ref, back_ref, cos_ref, sin_ref,
     send1, recv1, send2, recv2, send3, recv3, send4, recv4, send5, recv5,
     stat_out, stat_in, shuffle, query_t, grad_t, conv_t, taps_spec, mixed_spec,
-    send_sem, recv_sem, load_sem, store_sem,
+    send_sem, recv_sem, load_sem,
 ):
     loads = [
         pltpu.make_async_copy(source, target, load_sem.at[number])
@@ -80,15 +81,6 @@
             (query_in, query_ref), (grad_in, grad_ref), (first_in, first_ref),
             (ahead_in, ahead_ref), (back_in, back_ref), (last_in, last_ref),
             (cos_in, cos_ref), (sin_in, sin_ref),
-        ])
-    ]
-    for load in loads:
-        load.start()
-    mixer_store, dquery_store, dkey_store, dvalue_store, dtaps_store = stores = [
-        pltpu.make_async_copy(source, target, store_sem.at[number])
-        for number, (source, target) in enumerate([
-            (mixer_ref, mixer_out), (dquery_ref, dquery_out), (dkey_ref, dkey_out),
-            (dvalue_ref, dvalue_out), (dtaps_ref, dtaps_out),
         ])
     ]
     me = lax.axis_index("ctx")
@@ -134,20 +126,40 @@
 
     for_partners(greet_ctx)
     lax.fori_loop(1, m, greet_tp, 0)
+    for load in loads:
+        load.start()
+
+    def start(phase, source, target, peer):
+        pltpu.make_async_remote_copy(
+            src_ref=source.at[peer],
+            dst_ref=target.at[me],
+            send_sem=send_sem.at[phase],
+            recv_sem=recv_sem.at[phase],
+            device_id=(peer, mine),
+            device_id_type=MESH,
+        ).start()
 
     def exchange(phase, source, target):
-        def start(peer):
-            pltpu.make_async_remote_copy(
-                src_ref=source.at[peer],
-                dst_ref=target.at[me],
-                send_sem=send_sem.at[phase],
-                recv_sem=recv_sem.at[phase],
-                device_id=(peer, mine),
-                device_id_type=MESH,
-            ).start()
-
-        for_partners(start)
+        for_partners(functools.partial(start, phase, source, target))
         target[me] = source[me]
+
+    def deliver(phase, source, target, first, last):
+        def step(number, carry):
+            flip = lax.rem(number, 4) // 2
+            swap = lax.rem(number, 2)
+            peer = (
+                lax.rem(side + flip, 2) * (2 * chips)
+                + (number // 4) * 2
+                + lax.rem(core + swap, 2)
+            )
+
+            @pl.when(peer != me)
+            def _():
+                start(phase, source, target, peer)
+
+            return carry
+
+        lax.fori_loop(4 * first, 4 * last, step, 0)
 
     def arrived(phase, source, target):
         pltpu.make_async_copy(
@@ -251,8 +263,6 @@
     exchange(2, send3, recv3)
     mixer_ref[...] = (gated * inverse_rms).T.astype(BF16)
     dquery_ref[...] = (dgated * conv_t[...]).T.astype(BF16)
-    mixer_store.start()
-    dquery_store.start()
     arrived(2, send3, recv3)
 
     grads = stage_first(recv3[...])
@@ -262,23 +272,25 @@
         grads_real * taps_real + grads_imag * taps_imag,
         grads_imag * taps_real - grads_real * taps_imag,
     ).astype(BF16)
-    exchange(3, send4, recv4)
+    deliver(3, send4, recv4, 0, AHEAD)
+    recv4[me] = send4[me]
     mixed_real, mixed_imag = mixed_spec[:, :rows], mixed_spec[:, rows:]
     send5[...] = stage_last(
         grads_real * mixed_real + grads_imag * mixed_imag,
         grads_imag * mixed_real - grads_real * mixed_imag,
     ).astype(BF16)
-    exchange(4, send5, recv5)
+    deliver(4, send5, recv5, 0, AHEAD)
+    recv5[me] = send5[me]
+    for first in range(AHEAD, chips, STRIDE):
+        deliver(3, send4, recv4, first, min(first + STRIDE, chips))
+        deliver(4, send5, recv5, first, min(first + STRIDE, chips))
     arrived(3, send4, recv4)
 
     dmixed = recv4[...].astype(F32).reshape(cols, rows).T
     dkey_ref[...] = (dmixed * value_ref[...].astype(F32)).astype(BF16)
     dvalue_ref[...] = (dmixed * key_ref[...].astype(F32)).astype(BF16)
-    dkey_store.start()
-    dvalue_store.start()
     arrived(4, send5, recv5)
     dtaps_ref[...] = recv5[...].astype(F32).reshape(cols, rows).T.astype(BF16)
-    dtaps_store.start()
 
     sent(0, send1, recv1)
     sent(1, send2, recv2)
@@ -288,22 +300,15 @@
     pltpu.make_async_copy(
         stat_in.at[pl.ds(0, m - 1)], stat_in.at[pl.ds(0, m - 1)], send_sem.at[5]
     ).wait()
+
+
+def store_kernel(*refs):
+    sources, targets, sem = refs[:5], refs[5:10], refs[10]
+    stores = [
+        pltpu.make_async_copy(source, target, sem.at[number])
+        for number, (source, target) in enumerate(zip(sources, targets, strict=True))
+    ]
     for store in stores:
-        store.wait()
-
-
-def store_kernel(*refs):
-    sources, targets, middles, load_sem, store_sem = refs[:5], refs[5:10], refs[10:15], *refs[15:]
-    loads = [
-        pltpu.make_async_copy(sources[k], middles[k], load_sem.at[k]) for k in range(len(sources))
-    ]
-    stores = [
-        pltpu.make_async_copy(middles[k], targets[k], store_sem.at[k]) for k in range(len(sources))
-    ]
-    for load in loads:
-        load.start()
-    for load, store in zip(loads, stores, strict=True):
-        load.wait()
         store.start()
     for store in stores:
         store.wait()
@@ -322,11 +327,10 @@
     shapes = [jax.ShapeDtypeStruct((rows, cols), BF16)] * 5
     results = pl.pallas_call(
         functools.partial(kernel, n, m, cols * m, 1.0 / (math.sqrt(length) * length)),
-        out_shape=shapes,
+        out_shape=[pltpu.VMEM((rows, cols), BF16)] * 5,
         in_specs=[where] * 11,
-        out_specs=[where] * 5,
+        out_specs=[pl.BlockSpec(memory_space=pltpu.VMEM)] * 5,
         scratch_shapes=[
-            local, local, local, local, local,
             local, local, local, local, local,
             *[pltpu.VMEM(table.shape, table.dtype) for table in consts],
             two, two, one, one, one, one, one, one, one, one,
@@ -339,7 +343,6 @@
             pltpu.SemaphoreType.DMA((6,)),
             pltpu.SemaphoreType.DMA((6,)),
             pltpu.SemaphoreType.DMA((11,)),
-            pltpu.SemaphoreType.DMA((5,)),
         ],
         compiler_params=pltpu.CompilerParams(
             collective_id=0, has_side_effects=True, vmem_limit_bytes=VMEM_BYTES
@@ -348,10 +351,10 @@
     return pl.pallas_call(
         store_kernel,
         out_shape=shapes,
-        in_specs=[where] * 5,
+        in_specs=[pl.BlockSpec(memory_space=pltpu.VMEM)] * 5,
         out_specs=[where] * 5,
-        scratch_shapes=[local] * 5 + [pltpu.SemaphoreType.DMA((5,))] * 2,
-        compiler_params=pltpu.CompilerParams(vmem_limit_bytes=VMEM_BYTES),
+        scratch_shapes=[pltpu.SemaphoreType.DMA((5,))],
+        compiler_params=pltpu.CompilerParams(vmem_limit_bytes=8 * 1024 * 1024),
     )(*results)
 
 

time: 78.5 us -> 73.2 us (0.932)
  Pallas kernels: 77.7 us -> 72.4 us
    pallas_call x1, Pallas kernels: 75.8 us -> 71.6 us  [per_device(): pl.pallas_call(functools.partial(kernel, n, m, cols * m, 1.0 / (math.sqrt...]
    pallas_call x1, Pallas kernels: 1.91 us -> 0.87 us  [per_device(): pl.pallas_call(store_kernel, out_shape=shapes, in_specs=[pl.BlockSpec(mem...]
where the time goes in v3:
time: 73.2 us; the launch traced here: 73.1 us
  Pallas kernels  72.4 us (99%)
    pallas_call x1, Pallas kernels, per_device(): pl.pallas_call(functools.partial(kernel, n, m, cols * m, 1.0 / (math.sqrt...  71.6 us

profile of v3, /device:TPU:1, one launch (start us, length us, event | category | flops | bytes accessed | tf_op | source)
XLA Modules:
  0.0 73.1 jit_solution(17317179211974144241)
XLA Ops:
  0.6 71.6 %shard_map.146 = (bf16[128,512]{1,0:T(8,128)(2,1)S(1)}, bf16[128,512]{1,0:T(8,128)(2,1)S(1)}, bf16[128,512]{1,0:T(8,128)(2,1)S(1)}, bf16[128,512]{1,0:T(8,128)(2,1)S(1)}, bf16[128,512]{1,0:T(8,128)(2,1)S(1)}) custom-call(bf16[128,512]{1,0:T(8,128)(2,1)} %query_in.1, bf16[128,512]{1,0:T(8,128)(2,1)} %key_in.1, bf16[128,512]{1,0:T(8,128)(2,1)} %value_in.1, ...), custom_call_target="tpu_custom_call" | custom-call | tf_op jit(solution)/shard_map/pallas_call | solution.py:328
  72.2 0.9 %shard_map.147 = (bf16[128,512]{1,0:T(8,128)(2,1)}, bf16[128,512]{1,0:T(8,128)(2,1)}, bf16[128,512]{1,0:T(8,128)(2,1)}, bf16[128,512]{1,0:T(8,128)(2,1)}, bf16[128,512]{1,0:T(8,128)(2,1)}) custom-call(bf16[128,512]{1,0:T(8,128)(2,1)S(1)} %get-tuple-element.10.refs_0_, bf16[128,512]{1,0:T(8,128)(2,1)S(1)} %get-tuple-element.11.refs_1_, ...), custom_call_target="tpu_custom_call" | custom-call | tf_op jit(solution)/shard_map/pallas_call | solution.py:351

commit v4 on v3

--- a/solution.py
+++ b/solution.py
@@ -70,7 +70,8 @@
     mixer_ref, dquery_ref, dkey_ref, dvalue_ref, dtaps_ref,
     query_ref, key_ref, value_ref, taps_ref, grad_ref,
     first_ref, last_ref, ahead_ref, back_ref, cos_ref, sin_ref,
-    send1, recv1, send2, recv2, send3, recv3, send4, recv4, send5, recv5,
+    send1a, send1b, recv1a, recv1b, send2a, send2b, recv2a, recv2b,
+    send3a, send3b, recv3a, recv3b, send4, recv4, send5, recv5,
     stat_out, stat_in, shuffle, query_t, grad_t, conv_t, taps_spec, mixed_spec,
     send_sem, recv_sem, load_sem,
 ):
@@ -95,26 +96,25 @@
     place = lax.rem(me // 2, chips)
     core = lax.rem(me, 2)
 
-    def partner(step):
-        turn = step // 4
-        half = lax.rem(turn, 2)
-        far = jnp.where(half == 0, chips // 2 + turn // 2, chips // 2 - (turn + 1) // 2)
-        far = jnp.where(core == 0, far, chips - far)
-        flip = lax.rem(step, 4) // 2
-        swap = lax.rem(step, 2)
-        return (
-            lax.rem(side + flip, 2) * (2 * chips)
-            + lax.rem(place + far, chips) * 2
-            + lax.rem(core + swap, 2)
-        )
+    seats = [
+        lax.rem(side + flip, 2) * (2 * chips) + lax.rem(core + swap, 2)
+        for flip in range(2)
+        for swap in range(2)
+    ]
 
     def for_partners(body):
-        def step(number, carry):
-            body(partner(number))
+        def turn_step(turn, carry):
+            half = lax.rem(turn, 2)
+            far = jnp.where(half == 0, chips // 2 + turn // 2, chips // 2 - (turn + 1) // 2)
+            far = jnp.where(core == 0, far, chips - far)
+            there = 2 * lax.rem(place + far, chips)
+            for seat in seats:
+                body(seat + there)
             return carry
 
-        lax.fori_loop(0, n - 4, step, 0)
-        lax.fori_loop(n - 3, n, step, 0)
+        lax.fori_loop(0, chips - 1, turn_step, 0)
+        for seat in seats[1:]:
+            body(seat + 2 * place)
 
     def greet_ctx(peer):
         pl.semaphore_signal(barrier, inc=1, device_id=(peer, mine), device_id_type=MESH)
@@ -144,22 +144,17 @@
         target[me] = source[me]
 
     def deliver(phase, source, target, first, last):
-        def step(number, carry):
-            flip = lax.rem(number, 4) // 2
-            swap = lax.rem(number, 2)
-            peer = (
-                lax.rem(side + flip, 2) * (2 * chips)
-                + (number // 4) * 2
-                + lax.rem(core + swap, 2)
-            )
-
-            @pl.when(peer != me)
+        def step(there, carry):
+            for seat in seats[1:]:
+                start(phase, source, target, seat + 2 * there)
+
+            @pl.when(there != place)
             def _():
-                start(phase, source, target, peer)
+                start(phase, source, target, seats[0] + 2 * there)
 
             return carry
 
-        lax.fori_loop(4 * first, 4 * last, step, 0)
+        lax.fori_loop(first, last, step, 0)
 
     def arrived(phase, source, target):
         pltpu.make_async_copy(
@@ -172,14 +167,15 @@
         ).wait()
 
     def stage_first(blocks):
-        shuffle[...] = blocks.astype(F32).reshape(n * group, rows)
+        count = blocks.shape[1]
+        shuffle[pl.ds(0, n * count), :] = blocks.astype(F32).reshape(n * count, rows)
         columns = jnp.concatenate(
-            [shuffle[pl.ds(c, n, stride=group), :].astype(BF16) for c in range(group)], axis=1
+            [shuffle[pl.ds(c, n, stride=count), :].astype(BF16) for c in range(count)], axis=1
         )
         outer = dot(first_ref[...], jnp.concatenate([columns, columns], axis=0))
         cos, sin = cos_ref[...], sin_ref[...]
         turned = []
-        for c in range(group):
+        for c in range(count):
             real = outer[:n, c * rows : (c + 1) * rows]
             imag = outer[n:, c * rows : (c + 1) * rows]
             turned.append(
@@ -189,11 +185,12 @@
         return dot(jnp.concatenate([high, low, high], axis=1), ahead_ref[...])
 
     def stage_last(real, imag):
+        count = real.shape[0] // n
         high, low = split(jnp.concatenate([real, imag], axis=1))
         inner = dot(jnp.concatenate([high, low, high], axis=1), back_ref[...])
         cos, sin = cos_ref[...], sin_ref[...]
         turned = []
-        for c in range(group):
+        for c in range(count):
             real = inner[c * n : (c + 1) * n, :rows]
             imag = inner[c * n : (c + 1) * n, rows:]
             turned.append(
@@ -201,36 +198,51 @@
             )
         high, low = split(jnp.concatenate(turned, axis=1))
         outer = dot(last_ref[...], jnp.concatenate([high, low, high], axis=0))
-        for c in range(group):
-            shuffle[pl.ds(c, n, stride=group), :] = outer[:, c * rows : (c + 1) * rows] * scale
-        return shuffle[...].reshape(n, group, rows)
+        for c in range(count):
+            shuffle[pl.ds(c, n, stride=count), :] = outer[:, c * rows : (c + 1) * rows] * scale
+        return shuffle[pl.ds(0, n * count), :].reshape(n, count, rows)
 
     for load in loads[:3]:
         load.wait()
+    half = group // 2
     mixed = (key_ref[...].astype(F32) * value_ref[...].astype(F32)).astype(BF16).astype(F32)
-    send1[:, :group, :] = mixed.T.reshape(n, group, rows).astype(BF16)
-    send1[:, group:, :] = taps_ref[...].astype(F32).T.reshape(n, group, rows).astype(BF16)
+    mixed = mixed.T.reshape(n, group, rows)
+    taps = taps_ref[...].astype(F32).T.reshape(n, group, rows)
+    for part, send1 in enumerate((send1a, send1b)):
+        chosen = slice(part * half, (part + 1) * half)
+        send1[...] = jnp.concatenate([mixed[:, chosen], taps[:, chosen]], axis=1).astype(BF16)
     pl.semaphore_wait(barrier, n + m - 2)
-    exchange(0, send1, recv1)
+    exchange(0, send1a, recv1a)
+    exchange(5, send1b, recv1b)
     for load in loads[3:]:
         load.wait()
     query_t[...] = query_ref[...].astype(F32).T
     grad_t[...] = grad_ref[...].astype(F32).T
     stat_out[...] = jnp.zeros_like(stat_out)
-    arrived(0, send1, recv1)
-
-    mixed_spec[...] = stage_first(recv1[:, :group, :])
-    taps_spec[...] = stage_first(recv1[:, group:, :])
-    mixed_real, mixed_imag = mixed_spec[:, :rows], mixed_spec[:, rows:]
-    taps_real, taps_imag = taps_spec[:, :rows], taps_spec[:, rows:]
-    send2[...] = stage_last(
-        mixed_real * taps_real - mixed_imag * taps_imag,
-        mixed_real * taps_imag + mixed_imag * taps_real,
-    ).astype(BF16)
-    exchange(1, send2, recv2)
-    arrived(1, send2, recv2)
-
-    conv_t[...] = recv2[...].astype(F32).reshape(cols, rows)
+
+    for part, (phase1, send1, recv1, phase2, send2, recv2) in enumerate((
+        (0, send1a, recv1a, 1, send2a, recv2a),
+        (5, send1b, recv1b, 6, send2b, recv2b),
+    )):
+        arrived(phase1, send1, recv1)
+        spec = stage_first(recv1[...])
+        block = pl.ds(part * half * n, half * n)
+        mixed_spec[block, :] = spec[: half * n]
+        taps_spec[block, :] = spec[half * n :]
+        mixed_real, mixed_imag = spec[: half * n, :rows], spec[: half * n, rows:]
+        taps_real, taps_imag = spec[half * n :, :rows], spec[half * n :, rows:]
+        send2[...] = stage_last(
+            mixed_real * taps_real - mixed_imag * taps_imag,
+            mixed_real * taps_imag + mixed_imag * taps_real,
+        ).astype(BF16)
+        exchange(phase2, send2, recv2)
+    arrived(1, send2a, recv2a)
+    conv_first = recv2a[...].astype(F32)
+    arrived(6, send2b, recv2b)
+    conv_t[...] = jnp.concatenate([conv_first, recv2b[...].astype(F32)], axis=1).reshape(
+        cols, rows
+    )
+
     gated = query_t[...] * conv_t[...]
     stat_out[0:1, :] = jnp.sum(gated * gated, axis=0, keepdims=True)
     stat_out[1:2, :] = jnp.sum(grad_t[...] * gated, axis=0, keepdims=True)
@@ -240,8 +252,8 @@
         pltpu.make_async_remote_copy(
             src_ref=stat_out,
             dst_ref=stat_in.at[mine],
-            send_sem=send_sem.at[5],
-            recv_sem=recv_sem.at[5],
+            send_sem=send_sem.at[7],
+            recv_sem=recv_sem.at[7],
             device_id=(me, peer),
             device_id_type=MESH,
         ).start()
@@ -250,7 +262,7 @@
     lax.fori_loop(1, m, send_stats, 0)
     stat_in[mine] = stat_out[...]
     pltpu.make_async_copy(
-        stat_in.at[pl.ds(0, m - 1)], stat_in.at[pl.ds(0, m - 1)], recv_sem.at[5]
+        stat_in.at[pl.ds(0, m - 1)], stat_in.at[pl.ds(0, m - 1)], recv_sem.at[7]
     ).wait()
     totals = jnp.sum(stat_in[...], axis=0)
     inverse_rms = lax.rsqrt(totals[0:1, :] / width + EPS)
@@ -259,46 +271,54 @@
 
     gated = query_t[...] * conv_t[...]
     dgated = inverse_rms * grad_t[...] - weight * gated
-    send3[...] = (dgated * query_t[...]).astype(BF16).reshape(n, group, rows)
-    exchange(2, send3, recv3)
+    gconv = (dgated * query_t[...]).reshape(n, group, rows)
+    send3a[...] = gconv[:, :half].astype(BF16)
+    exchange(2, send3a, recv3a)
+    send3b[...] = gconv[:, half:].astype(BF16)
+    exchange(8, send3b, recv3b)
     mixer_ref[...] = (gated * inverse_rms).T.astype(BF16)
     dquery_ref[...] = (dgated * conv_t[...]).T.astype(BF16)
-    arrived(2, send3, recv3)
-
-    grads = stage_first(recv3[...])
-    grads_real, grads_imag = grads[:, :rows], grads[:, rows:]
-    taps_real, taps_imag = taps_spec[:, :rows], taps_spec[:, rows:]
-    send4[...] = stage_last(
-        grads_real * taps_real + grads_imag * taps_imag,
-        grads_imag * taps_real - grads_real * taps_imag,
-    ).astype(BF16)
-    deliver(3, send4, recv4, 0, AHEAD)
-    recv4[me] = send4[me]
-    mixed_real, mixed_imag = mixed_spec[:, :rows], mixed_spec[:, rows:]
-    send5[...] = stage_last(
-        grads_real * mixed_real + grads_imag * mixed_imag,
-        grads_imag * mixed_real - grads_real * mixed_imag,
-    ).astype(BF16)
-    deliver(4, send5, recv5, 0, AHEAD)
-    recv5[me] = send5[me]
+
+    for part, (phase3, send3, recv3, phase4, send, recv) in enumerate((
+        (2, send3a, recv3a, 3, send4, recv4),
+        (8, send3b, recv3b, 4, send5, recv5),
+    )):
+        arrived(phase3, send3, recv3)
+        grads = stage_first(recv3[...])
+        grads = jnp.concatenate([grads, grads], axis=0)
+        block = pl.ds(part * half * n, half * n)
+        others = jnp.concatenate([taps_spec[block, :], mixed_spec[block, :]], axis=0)
+        grads_real, grads_imag = grads[:, :rows], grads[:, rows:]
+        other_real, other_imag = others[:, :rows], others[:, rows:]
+        send[...] = stage_last(
+            grads_real * other_real + grads_imag * other_imag,
+            grads_imag * other_real - grads_real * other_imag,
+        ).astype(BF16)
+        deliver(phase4, send, recv, 0, AHEAD)
+        recv[me] = send[me]
     for first in range(AHEAD, chips, STRIDE):
         deliver(3, send4, recv4, first, min(first + STRIDE, chips))
         deliver(4, send5, recv5, first, min(first + STRIDE, chips))
     arrived(3, send4, recv4)
-
-    dmixed = recv4[...].astype(F32).reshape(cols, rows).T
+    arrived(4, send5, recv5)
+
+    dmixed = jnp.concatenate([recv4[:, :half, :], recv5[:, :half, :]], axis=1)
+    dmixed = dmixed.astype(F32).reshape(cols, rows).T
     dkey_ref[...] = (dmixed * value_ref[...].astype(F32)).astype(BF16)
     dvalue_ref[...] = (dmixed * key_ref[...].astype(F32)).astype(BF16)
-    arrived(4, send5, recv5)
-    dtaps_ref[...] = recv5[...].astype(F32).reshape(cols, rows).T.astype(BF16)
-
-    sent(0, send1, recv1)
-    sent(1, send2, recv2)
-    sent(2, send3, recv3)
+    dtaps = jnp.concatenate([recv4[:, half:, :], recv5[:, half:, :]], axis=1)
+    dtaps_ref[...] = dtaps.astype(F32).reshape(cols, rows).T.astype(BF16)
+
+    sent(0, send1a, recv1a)
+    sent(5, send1b, recv1b)
+    sent(1, send2a, recv2a)
+    sent(6, send2b, recv2b)
+    sent(2, send3a, recv3a)
+    sent(8, send3b, recv3b)
     sent(3, send4, recv4)
     sent(4, send5, recv5)
     pltpu.make_async_copy(
-        stat_in.at[pl.ds(0, m - 1)], stat_in.at[pl.ds(0, m - 1)], send_sem.at[5]
+        stat_in.at[pl.ds(0, m - 1)], stat_in.at[pl.ds(0, m - 1)], send_sem.at[7]
     ).wait()
 
 
@@ -321,7 +341,7 @@
     consts = [jnp.asarray(table) for table in tables(n, rows)]
     where = pl.BlockSpec(memory_space=pl.ANY)
     one = pltpu.VMEM((n, group, rows), BF16)
-    two = pltpu.VMEM((n, 2 * group, rows), BF16)
+    part = pltpu.VMEM((n, group // 2, rows), BF16)
     wide = pltpu.VMEM((cols, rows), F32)
     local = pltpu.VMEM((rows, cols), BF16)
     shapes = [jax.ShapeDtypeStruct((rows, cols), BF16)] * 5
@@ -333,15 +353,15 @@
         scratch_shapes=[
             local, local, local, local, local,
             *[pltpu.VMEM(table.shape, table.dtype) for table in consts],
-            two, two, one, one, one, one, one, one, one, one,
+            one, one, one, one, part, part, part, part, part, part, part, part, one, one, one, one,
             pltpu.VMEM((8, rows), F32),
             pltpu.VMEM((m, 8, rows), F32),
             pltpu.VMEM((n * group, rows), F32),
             wide, wide, wide,
             pltpu.VMEM((n * group, 2 * rows), F32),
             pltpu.VMEM((n * group, 2 * rows), F32),
-            pltpu.SemaphoreType.DMA((6,)),
-            pltpu.SemaphoreType.DMA((6,)),
+            pltpu.SemaphoreType.DMA((9,)),
+            pltpu.SemaphoreType.DMA((9,)),
             pltpu.SemaphoreType.DMA((11,)),
         ],
         compiler_params=pltpu.CompilerParams(

time: 73.2 us -> 71 us (0.970)
  Pallas kernels: 72.4 us -> 69.5 us
    pallas_call x1, Pallas kernels: 71.6 us -> 68.6 us  [per_device(): pl.pallas_call(functools.partial(kernel, n, m, cols * m, 1.0 / (math.sqrt...]
where the time goes in v4:
time: 71 us; the launch traced here: 70.2 us
  Pallas kernels  69.5 us (98%)
    pallas_call x1, Pallas kernels, per_device(): pl.pallas_call(functools.partial(kernel, n, m, cols * m, 1.0 / (math.sqrt...  68.6 us

profile of v4, /device:TPU:1, one launch (start us, length us, event | category | flops | bytes accessed | tf_op | source)
XLA Modules:
  0.0 70.2 jit_solution(10249098011906508946)
XLA Ops:
  0.6 68.6 %shard_map.146 = (bf16[128,512]{1,0:T(8,128)(2,1)S(1)}, bf16[128,512]{1,0:T(8,128)(2,1)S(1)}, bf16[128,512]{1,0:T(8,128)(2,1)S(1)}, bf16[128,512]{1,0:T(8,128)(2,1)S(1)}, bf16[128,512]{1,0:T(8,128)(2,1)S(1)}) custom-call(bf16[128,512]{1,0:T(8,128)(2,1)} %query_in.1, bf16[128,512]{1,0:T(8,128)(2,1)} %key_in.1, bf16[128,512]{1,0:T(8,128)(2,1)} %value_in.1, ...), custom_call_target="tpu_custom_call" | custom-call | tf_op jit(solution)/shard_map/pallas_call | solution.py:348
  69.3 0.9 %shard_map.147 = (bf16[128,512]{1,0:T(8,128)(2,1)}, bf16[128,512]{1,0:T(8,128)(2,1)}, bf16[128,512]{1,0:T(8,128)(2,1)}, bf16[128,512]{1,0:T(8,128)(2,1)}, bf16[128,512]{1,0:T(8,128)(2,1)}) custom-call(bf16[128,512]{1,0:T(8,128)(2,1)S(1)} %get-tuple-element.10.refs_0_, bf16[128,512]{1,0:T(8,128)(2,1)S(1)} %get-tuple-element.11.refs_1_, ...), custom_call_target="tpu_custom_call" | custom-call | tf_op jit(solution)/shard_map/pallas_call | solution.py:371

commit v5 on v4

--- a/solution.py
+++ b/solution.py
@@ -14,6 +14,7 @@
 F32 = jnp.float32
 BF16 = jnp.bfloat16
 EPS = 1e-05
+PARTS = (4, 4)
 AHEAD = 4
 STRIDE = 2
 VMEM_BYTES = 63 * 1024 * 1024
@@ -64,14 +65,13 @@
 
 
 def kernel(
-    n, m, width, scale,
+    n, m, parts, width, scale,
     query_in, key_in, value_in, taps_in, grad_in,
     first_in, last_in, ahead_in, back_in, cos_in, sin_in,
     mixer_ref, dquery_ref, dkey_ref, dvalue_ref, dtaps_ref,
     query_ref, key_ref, value_ref, taps_ref, grad_ref,
     first_ref, last_ref, ahead_ref, back_ref, cos_ref, sin_ref,
-    send1a, send1b, recv1a, recv1b, send2a, send2b, recv2a, recv2b,
-    send3a, send3b, recv3a, recv3b, send4, recv4, send5, recv5,
+    buffers,
     stat_out, stat_in, shuffle, query_t, grad_t, conv_t, taps_spec, mixed_spec,
     send_sem, recv_sem, load_sem,
 ):
@@ -202,58 +202,67 @@
             shuffle[pl.ds(c, n, stride=count), :] = outer[:, c * rows : (c + 1) * rows] * scale
         return shuffle[pl.ds(0, n * count), :].reshape(n, count, rows)
 
+    pieces = []
+    at = 0
+    for number, count in enumerate(parts):
+        phases = [
+            (4 * number + step, buffers[8 * number + 2 * step], buffers[8 * number + 2 * step + 1])
+            for step in range(4)
+        ]
+        pieces.append((slice(at * n, (at + count) * n), count, phases))
+        at += count
+
     for load in loads[:3]:
         load.wait()
-    half = group // 2
-    mixed = (key_ref[...].astype(F32) * value_ref[...].astype(F32)).astype(BF16).astype(F32)
-    mixed = mixed.T.reshape(n, group, rows)
-    taps = taps_ref[...].astype(F32).T.reshape(n, group, rows)
-    for part, send1 in enumerate((send1a, send1b)):
-        chosen = slice(part * half, (part + 1) * half)
-        send1[...] = jnp.concatenate([mixed[:, chosen], taps[:, chosen]], axis=1).astype(BF16)
+    mixed = (key_ref[...].astype(F32) * value_ref[...].astype(F32)).astype(BF16).astype(F32).T
+    taps = taps_ref[...].astype(F32).T
+    for rows_here, count, phases in pieces:
+        block = (n, count, rows)
+        phases[0][1][...] = jnp.concatenate(
+            [mixed[rows_here].reshape(block), taps[rows_here].reshape(block)], axis=1
+        ).astype(BF16)
     pl.semaphore_wait(barrier, n + m - 2)
-    exchange(0, send1a, recv1a)
-    exchange(5, send1b, recv1b)
+    for _, _, phases in pieces:
+        exchange(*phases[0])
     for load in loads[3:]:
         load.wait()
     query_t[...] = query_ref[...].astype(F32).T
     grad_t[...] = grad_ref[...].astype(F32).T
     stat_out[...] = jnp.zeros_like(stat_out)
 
-    for part, (phase1, send1, recv1, phase2, send2, recv2) in enumerate((
-        (0, send1a, recv1a, 1, send2a, recv2a),
-        (5, send1b, recv1b, 6, send2b, recv2b),
-    )):
-        arrived(phase1, send1, recv1)
-        spec = stage_first(recv1[...])
-        block = pl.ds(part * half * n, half * n)
-        mixed_spec[block, :] = spec[: half * n]
-        taps_spec[block, :] = spec[half * n :]
-        mixed_real, mixed_imag = spec[: half * n, :rows], spec[: half * n, rows:]
-        taps_real, taps_imag = spec[half * n :, :rows], spec[half * n :, rows:]
-        send2[...] = stage_last(
+    for rows_here, count, phases in pieces:
+        arrived(*phases[0])
+        spec = stage_first(phases[0][2][...])
+        mixed_here, taps_here = spec[: count * n], spec[count * n :]
+        mixed_spec[rows_here, :] = mixed_here
+        taps_spec[rows_here, :] = taps_here
+        mixed_real, mixed_imag = mixed_here[:, :rows], mixed_here[:, rows:]
+        taps_real, taps_imag = taps_here[:, :rows], taps_here[:, rows:]
+        phases[1][1][...] = stage_last(
             mixed_real * taps_real - mixed_imag * taps_imag,
             mixed_real * taps_imag + mixed_imag * taps_real,
         ).astype(BF16)
-        exchange(phase2, send2, recv2)
-    arrived(1, send2a, recv2a)
-    conv_first = recv2a[...].astype(F32)
-    arrived(6, send2b, recv2b)
-    conv_t[...] = jnp.concatenate([conv_first, recv2b[...].astype(F32)], axis=1).reshape(
-        cols, rows
-    )
-
-    gated = query_t[...] * conv_t[...]
-    stat_out[0:1, :] = jnp.sum(gated * gated, axis=0, keepdims=True)
-    stat_out[1:2, :] = jnp.sum(grad_t[...] * gated, axis=0, keepdims=True)
+        exchange(*phases[1])
+
+    square_sum = jnp.zeros((1, rows), F32)
+    dot_sum = jnp.zeros((1, rows), F32)
+    for rows_here, count, phases in pieces:
+        arrived(*phases[1])
+        conv_here = phases[1][2][...].astype(F32).reshape(n * count, rows)
+        conv_t[rows_here, :] = conv_here
+        gated = query_t[rows_here, :] * conv_here
+        square_sum += jnp.sum(gated * gated, axis=0, keepdims=True)
+        dot_sum += jnp.sum(grad_t[rows_here, :] * gated, axis=0, keepdims=True)
+    stat_out[0:1, :] = square_sum
+    stat_out[1:2, :] = dot_sum
 
     def send_stats(step, carry):
         peer = lax.rem(mine + step, m)
         pltpu.make_async_remote_copy(
             src_ref=stat_out,
             dst_ref=stat_in.at[mine],
-            send_sem=send_sem.at[7],
-            recv_sem=recv_sem.at[7],
+            send_sem=send_sem.at[4 * len(parts)],
+            recv_sem=recv_sem.at[4 * len(parts)],
             device_id=(me, peer),
             device_id_type=MESH,
         ).start()
@@ -262,63 +271,53 @@
     lax.fori_loop(1, m, send_stats, 0)
     stat_in[mine] = stat_out[...]
     pltpu.make_async_copy(
-        stat_in.at[pl.ds(0, m - 1)], stat_in.at[pl.ds(0, m - 1)], recv_sem.at[7]
+        stat_in.at[pl.ds(0, m - 1)], stat_in.at[pl.ds(0, m - 1)], recv_sem.at[4 * len(parts)]
     ).wait()
     totals = jnp.sum(stat_in[...], axis=0)
     inverse_rms = lax.rsqrt(totals[0:1, :] / width + EPS)
     dots = totals[1:2, :] / width
     weight = inverse_rms * inverse_rms * inverse_rms * dots
 
+    for rows_here, count, phases in pieces:
+        query_here, conv_here = query_t[rows_here, :], conv_t[rows_here, :]
+        dgated = inverse_rms * grad_t[rows_here, :] - weight * (query_here * conv_here)
+        phases[2][1][...] = (dgated * query_here).astype(BF16).reshape(n, count, rows)
+        exchange(*phases[2])
     gated = query_t[...] * conv_t[...]
     dgated = inverse_rms * grad_t[...] - weight * gated
-    gconv = (dgated * query_t[...]).reshape(n, group, rows)
-    send3a[...] = gconv[:, :half].astype(BF16)
-    exchange(2, send3a, recv3a)
-    send3b[...] = gconv[:, half:].astype(BF16)
-    exchange(8, send3b, recv3b)
     mixer_ref[...] = (gated * inverse_rms).T.astype(BF16)
     dquery_ref[...] = (dgated * conv_t[...]).T.astype(BF16)
 
-    for part, (phase3, send3, recv3, phase4, send, recv) in enumerate((
-        (2, send3a, recv3a, 3, send4, recv4),
-        (8, send3b, recv3b, 4, send5, recv5),
-    )):
-        arrived(phase3, send3, recv3)
-        grads = stage_first(recv3[...])
+    for rows_here, _, phases in pieces:
+        arrived(*phases[2])
+        grads = stage_first(phases[2][2][...])
         grads = jnp.concatenate([grads, grads], axis=0)
-        block = pl.ds(part * half * n, half * n)
-        others = jnp.concatenate([taps_spec[block, :], mixed_spec[block, :]], axis=0)
+        others = jnp.concatenate([taps_spec[rows_here, :], mixed_spec[rows_here, :]], axis=0)
         grads_real, grads_imag = grads[:, :rows], grads[:, rows:]
         other_real, other_imag = others[:, :rows], others[:, rows:]
-        send[...] = stage_last(
+        phases[3][1][...] = stage_last(
             grads_real * other_real + grads_imag * other_imag,
             grads_imag * other_real - grads_real * other_imag,
         ).astype(BF16)
-        deliver(phase4, send, recv, 0, AHEAD)
-        recv[me] = send[me]
+        deliver(*phases[3], 0, AHEAD)
+        phases[3][2][me] = phases[3][1][me]
     for first in range(AHEAD, chips, STRIDE):
-        deliver(3, send4, recv4, first, min(first + STRIDE, chips))
-        deliver(4, send5, recv5, first, min(first + STRIDE, chips))
-    arrived(3, send4, recv4)
-    arrived(4, send5, recv5)
-
-    dmixed = jnp.concatenate([recv4[:, :half, :], recv5[:, :half, :]], axis=1)
-    dmixed = dmixed.astype(F32).reshape(cols, rows).T
-    dkey_ref[...] = (dmixed * value_ref[...].astype(F32)).astype(BF16)
-    dvalue_ref[...] = (dmixed * key_ref[...].astype(F32)).astype(BF16)
-    dtaps = jnp.concatenate([recv4[:, half:, :], recv5[:, half:, :]], axis=1)
-    dtaps_ref[...] = dtaps.astype(F32).reshape(cols, rows).T.astype(BF16)
-
-    sent(0, send1a, recv1a)
-    sent(5, send1b, recv1b)
-    sent(1, send2a, recv2a)
-    sent(6, send2b, recv2b)
-    sent(2, send3a, recv3a)
-    sent(8, send3b, recv3b)
-    sent(3, send4, recv4)
-    sent(4, send5, recv5)
+        for _, _, phases in pieces:
+            deliver(*phases[3], first, min(first + STRIDE, chips))
+
+    for rows_here, count, phases in pieces:
+        arrived(*phases[3])
+        dmixed = phases[3][2][:, :count, :].astype(F32).reshape(n * count, rows).T
+        dkey_ref[:, rows_here] = (dmixed * value_ref[:, rows_here].astype(F32)).astype(BF16)
+        dvalue_ref[:, rows_here] = (dmixed * key_ref[:, rows_here].astype(F32)).astype(BF16)
+        dtaps = phases[3][2][:, count:, :].astype(F32).reshape(n * count, rows).T
+        dtaps_ref[:, rows_here] = dtaps.astype(BF16)
+
+    for _, _, phases in pieces:
+        for exchanged in phases:
+            sent(*exchanged)
     pltpu.make_async_copy(
-        stat_in.at[pl.ds(0, m - 1)], stat_in.at[pl.ds(0, m - 1)], send_sem.at[7]
+        stat_in.at[pl.ds(0, m - 1)], stat_in.at[pl.ds(0, m - 1)], send_sem.at[4 * len(parts)]
     ).wait()
 
 
@@ -340,28 +339,32 @@
     length = rows * n
     consts = [jnp.asarray(table) for table in tables(n, rows)]
     where = pl.BlockSpec(memory_space=pl.ANY)
-    one = pltpu.VMEM((n, group, rows), BF16)
-    part = pltpu.VMEM((n, group // 2, rows), BF16)
+    parts = PARTS
+    heights = [
+        height
+        for count in parts
+        for height in (2 * count, 2 * count, count, count, count, count, 2 * count, 2 * count)
+    ]
     wide = pltpu.VMEM((cols, rows), F32)
     local = pltpu.VMEM((rows, cols), BF16)
     shapes = [jax.ShapeDtypeStruct((rows, cols), BF16)] * 5
     results = pl.pallas_call(
-        functools.partial(kernel, n, m, cols * m, 1.0 / (math.sqrt(length) * length)),
+        functools.partial(kernel, n, m, parts, cols * m, 1.0 / (math.sqrt(length) * length)),
         out_shape=[pltpu.VMEM((rows, cols), BF16)] * 5,
         in_specs=[where] * 11,
         out_specs=[pl.BlockSpec(memory_space=pltpu.VMEM)] * 5,
         scratch_shapes=[
             local, local, local, local, local,
             *[pltpu.VMEM(table.shape, table.dtype) for table in consts],
-            one, one, one, one, part, part, part, part, part, part, part, part, one, one, one, one,
+            [pltpu.VMEM((n, height, rows), BF16) for height in heights],
             pltpu.VMEM((8, rows), F32),
             pltpu.VMEM((m, 8, rows), F32),
             pltpu.VMEM((n * group, rows), F32),
             wide, wide, wide,
             pltpu.VMEM((n * group, 2 * rows), F32),
             pltpu.VMEM((n * group, 2 * rows), F32),
-            pltpu.SemaphoreType.DMA((9,)),
-            pltpu.SemaphoreType.DMA((9,)),
+            pltpu.SemaphoreType.DMA((4 * len(parts) + 1,)),
+            pltpu.SemaphoreType.DMA((4 * len(parts) + 1,)),
             pltpu.SemaphoreType.DMA((11,)),
         ],
         compiler_params=pltpu.CompilerParams(

time: 71 us -> 70.8 us (level); the launches traced: 70.2 us -> 70.7 us
  no operation moved by 1% of the time
where the time goes in v5:
time: 70.8 us; the launch traced here: 70.7 us
  Pallas kernels  70 us (99%)
    pallas_call x1, Pallas kernels, per_device(): pl.pallas_call(functools.partial(kernel, n, m, parts, cols * m, 1.0 / (ma...  69.2 us

profile of v5, /device:TPU:1, one launch (start us, length us, event | category | flops | bytes accessed | tf_op | source)
XLA Modules:
  0.0 70.7 jit_solution(15418020023248870346)
XLA Ops:
  0.6 69.2 %shard_map.146 = (bf16[128,512]{1,0:T(8,128)(2,1)S(1)}, bf16[128,512]{1,0:T(8,128)(2,1)S(1)}, bf16[128,512]{1,0:T(8,128)(2,1)S(1)}, bf16[128,512]{1,0:T(8,128)(2,1)S(1)}, bf16[128,512]{1,0:T(8,128)(2,1)S(1)}) custom-call(bf16[128,512]{1,0:T(8,128)(2,1)} %query_in.1, bf16[128,512]{1,0:T(8,128)(2,1)} %key_in.1, bf16[128,512]{1,0:T(8,128)(2,1)} %value_in.1, ...), custom_call_target="tpu_custom_call" | custom-call | tf_op jit(solution)/shard_map/pallas_call | solution.py:351
  69.8 0.9 %shard_map.147 = (bf16[128,512]{1,0:T(8,128)(2,1)}, bf16[128,512]{1,0:T(8,128)(2,1)}, bf16[128,512]{1,0:T(8,128)(2,1)}, bf16[128,512]{1,0:T(8,128)(2,1)}, bf16[128,512]{1,0:T(8,128)(2,1)}) custom-call(bf16[128,512]{1,0:T(8,128)(2,1)S(1)} %get-tuple-element.10.refs_0_, bf16[128,512]{1,0:T(8,128)(2,1)S(1)} %get-tuple-element.11.refs_1_, ...), custom_call_target="tpu_custom_call" | custom-call | tf_op jit(solution)/shard_map/pallas_call | solution.py:374
